TPU v7x, 32 devices: a whole 2x2x4 slice. The times are simulated.
32 devices in a mesh: row: 4 (over y, core), col: 2 (over x), layer: 4 (over z).
Axes of the slice: x: 2, y: 2, z: 4, core: 2. Of those that a mesh axis runs over, the one named last changes fastest.
Arguments:
- blocks: bfloat16 [704, 128, 128], P(('col', 'layer')), may hold values from -6 to 6
- block_aux: int32 [704], P(('col', 'layer')), may hold values from 0 to 23
- block_row: int32 [704], P(('col', 'layer')), may hold values from 0 to 1, as said below
- block_col: int32 [704], P(('col', 'layer')), may hold values from 0 to 159, as said below
- extents: int32 [704], P(('col', 'layer')), may hold values from 32 to 128
- occ_green: bfloat16 [20480, 256], P('layer', 'row'), may hold values from -0.01171875 to 0.01171875
- virt_green: bfloat16 [20480, 256], P('layer', 'row'), may hold values from -0.01171875 to 0.01171875
Outputs:
- chi: float32 [24, 24], replicated
Inputs may be any that keep to these rules, and one draw needn't show every extreme that they name: block_row[n] numbers the block of 128 window functions that tile n covers. The owner of tile n is the pair (block_row[n], block_col[n] // 40). Within each device's share of 88 consecutive entries no owner appears more than 12 times, and one owner, the same for every share, appears exactly 12 times in every share.
All inputs are finite; a program needn't handle non-finite values.
Results may differ from a plain program's by a relative error of at most 0.0003.
Values may be sent and summed in bfloat16 or wider, within the bound.
A program may use at most 192 MiB of HBM per device.

v0:
```python
import jax
import jax.numpy as jnp
from jax import lax
from jax.sharding import PartitionSpec as P

NP = 24


def on_device(blocks, block_aux, block_row, block_col, extents, occ_green, virt_green):
    row_count = lax.axis_size("row")
    col_count = lax.axis_size("col")
    layer_count = lax.axis_size("layer")
    held_count = blocks.shape[0]
    tile_side = blocks.shape[1]
    aux_count = NP
    owner_count = col_count * layer_count
    capacity = max(2, held_count // owner_count + 1)
    layer_blocks = occ_green.shape[0] // tile_side
    columns = jnp.arange(tile_side, dtype=jnp.int32)
    masked_tiles = jnp.where(
        columns[None, None, :] < extents[:, None, None], blocks, jnp.zeros((), blocks.dtype)
    )
    layer_of = block_col // layer_blocks
    target = block_row * layer_count + layer_of
    kept_col = block_col - layer_of * layer_blocks
    marked = (target[:, None] == jnp.arange(owner_count, dtype=jnp.int32)[None, :]).astype(
        jnp.int32
    )
    earlier = jnp.cumsum(marked, axis=0) - marked
    placed = target * capacity + jnp.sum(earlier * marked, axis=1)
    send_tiles = (
        jnp.zeros((owner_count * capacity, tile_side, tile_side), blocks.dtype)
        .at[placed]
        .set(masked_tiles)
    )
    send_meta = (
        jnp.zeros((owner_count * capacity, 2), jnp.int32)
        .at[placed]
        .set(jnp.stack([block_aux, kept_col], axis=1))
    )
    send_tiles = send_tiles.reshape(col_count, layer_count, capacity, tile_side, tile_side)
    send_meta = send_meta.reshape(col_count, layer_count, capacity, 2)
    total_slots = col_count * layer_count * capacity
    got_tiles, got_meta = (
        lax.all_to_all(
            send_tiles.reshape(total_slots, tile_side, tile_side),
            ("col", "layer"),
            split_axis=0,
            concat_axis=0,
            tiled=True,
        ),
        lax.all_to_all(
            send_meta.reshape(total_slots, 2),
            ("col", "layer"),
            split_axis=0,
            concat_axis=0,
            tiled=True,
        ),
    )
    group_size = col_count * capacity
    got_tiles = got_tiles.reshape(layer_count, group_size, tile_side, tile_side)
    got_meta = got_meta.reshape(layer_count, group_size, 2)
    occ_cols, virt_cols = (occ_green, virt_green)
    width_here = occ_cols.shape[1]
    offsets = jnp.arange(tile_side, dtype=jnp.int32)

    def add_group(totals, record):
        occ_total, virt_total = totals
        tile_group, meta_group = record
        row_index = meta_group[:, 1][:, None] * tile_side + offsets[None, :]
        occ_rows = occ_cols[row_index]
        virt_rows = virt_cols[row_index]
        occ_term = jnp.einsum(
            "gsv,gls->gvl", occ_rows, tile_group, preferred_element_type=jnp.float32
        )
        virt_term = jnp.einsum(
            "gvs,gsl->gvl", tile_group, virt_rows, preferred_element_type=jnp.float32
        )
        aux_index = meta_group[:, 0]
        return (
            (occ_total.at[aux_index].add(occ_term), virt_total.at[aux_index].add(virt_term)),
            None,
        )

    start_totals = (
        jnp.zeros((aux_count, width_here, tile_side), jnp.float32),
        jnp.zeros((aux_count, tile_side, width_here), jnp.float32),
    )
    (occ_total, virt_total), _ = lax.scan(add_group, start_totals, (got_tiles, got_meta))
    occ_done, virt_done = (
        lax.psum_scatter(occ_total, "layer", scatter_dimension=1, tiled=True),
        lax.psum_scatter(virt_total, "layer", scatter_dimension=2, tiled=True),
    )
    mesh_count = row_count * layer_count
    thin_rows = tile_side // mesh_count
    stack_count = mesh_count // col_count
    narrow = occ_done.shape[1]
    occ_five = occ_done.reshape(aux_count, 1, col_count, thin_rows, tile_side)
    virt_five = virt_done.reshape(aux_count, stack_count, col_count, thin_rows, narrow)
    occ_moved, virt_moved = (
        lax.all_to_all(occ_five, "col", split_axis=2, concat_axis=1, tiled=True),
        lax.all_to_all(virt_five, "col", split_axis=2, concat_axis=1, tiled=True),
    )
    virt_four = virt_moved.reshape(aux_count, mesh_count, thin_rows, narrow)
    virt_back = lax.all_to_all(virt_four, ("row", "layer"), split_axis=1, concat_axis=3, tiled=True)
    occ_final = occ_moved.reshape(aux_count, col_count, thin_rows, tile_side)
    virt_final = virt_back.reshape(aux_count, thin_rows, col_count, tile_side)
    chi_part = jnp.einsum(
        "pcji,qjci->pq",
        occ_final,
        virt_final,
        precision=lax.Precision.HIGHEST,
        preferred_element_type=jnp.float32,
    )
    return lax.psum(chi_part, ("row", "col", "layer"))


def solution(mesh):
    in_specs = (
        P(("col", "layer"), None, None),
        P(("col", "layer")),
        P(("col", "layer")),
        P(("col", "layer")),
        P(("col", "layer")),
        P("layer", "row"),
        P("layer", "row"),
    )
    out_specs = P()
    return jax.shard_map(
        on_device, mesh=mesh, in_specs=in_specs, out_specs=out_specs, check_vma=False
    )
```

profile of v0, /device:TPU:0, one launch (start us, length us, event | category | flops | bytes accessed | tf_op | source)
XLA Modules:
  0.0 426.9 jit_solution(1433548081200329209)
XLA Ops:
  10.6 7.3 %all-to-all-start = ((s32[8,12,2]{1,2,0:T(2,128)}), s32[8,12,2]{1,2,0:T(2,128)S(1)}, u32[]{:S(2)}, u32[]{:S(2)}) async-start(s32[8,12,2]{1,2,0:T(2,128)} %copy.29), calls=%async_computation | async-start | bytes 16384 | tf_op jit(solution)/shard_map/all_to_all | solution.py:52
  18.6 2.1 broadcast_select_fusion
  20.7 2.5 broadcast_in_dim.41
  23.1 12.7 %scatter_fusion.2 = bf16[96,128,128]{2,1,0:T(8,128)(2,1)} fusion(bf16[96,128,128]{2,1,0:T(8,128)(2,1)} %broadcast_in_dim.41, s32[88]{0:T(128)S(1)} %compare_select_fusion.2, bf16[88,128,128]{2,1,0:T(8,128)(2,1)S(1)} %broadcast_select_fusion), kind=kCustom, calls=%fused_computation.5 | custom fusion | bytes 8651104 | tf_op jit(solution)/shard_map/scatter | solution.py:34
  35.8 6.1 %all-to-all-start.1 = ((bf16[96,128,128]{2,1,0:T(8,128)(2,1)}), bf16[96,128,128]{2,1,0:T(8,128)(2,1)}, u32[]{:S(2)}, u32[]{:S(2)}) async-start(bf16[96,128,128]{2,1,0:T(8,128)(2,1)} %scatter_fusion.2), calls=%async_computation.1 | async-start | bytes 6291456 | tf_op jit(solution)/shard_map/all_to_all | solution.py:45
  43.6 69.4 %all-to-all-done.1 = bf16[96,128,128]{2,1,0:T(8,128)(2,1)} async-done(((bf16[96,128,128]{2,1,0:T(8,128)(2,1)}), bf16[96,128,128]{2,1,0:T(8,128)(2,1)}, u32[]{:S(2)}, u32[]{:S(2)}) %all-to-all-start.1) | async-done | bytes 3145760 | tf_op jit(solution)/shard_map/all_to_all | solution.py:45
  113.0 1.0 broadcast_in_dim.22
  114.0 1.0 broadcast_in_dim.38
  115.0 147.1 %while.13 = (s32[]{:T(128)}, f32[24,64,128]{2,1,0:T(8,128)}, f32[24,128,64]{1,2,0:T(8,128)}, s32[4,24,2]{1,0,2:T(4,128)S(1)}, bf16[5120,64]{1,0:T(8,128)(2,1)S(1...) while((s32[]{:T(128)}, f32[24,64,128]{2,1,0:T(8,128)}, ...), condition=%wide.region_7.8_spmd.clone, body=%wide.region_4.7_spmd.clone.sunk | while | flops 101071968 | bytes 11049081 | solution.py:89
  115.1 11.4 %gather_fusion.1 = bf16[3072,64]{1,0:T(8,128)(2,1)} fusion(bf16[5120,64]{1,0:T(8,128)(2,1)S(1)} %get-tuple-element.174, s32[3072]{0:T(1024)S(1)} %fusion.31), kind=kCustom, calls=%fused_computation.1.clone.clone.1 | custom fusion | bytes 798720 | tf_op jit(solution)/shard_map/while/body/eval_jaxpr/gather | solution.py:72
  126.5 2.0 fusion.33
  128.5 4.8 %scatter_fusion.1 = f32[24,128,64]{1,2,0:T(8,128)} fusion(f32[24,128,64]{1,2,0:T(8,128)} %get-tuple-element.162, s32[24]{0:T(128)S(1)} %get-tuple-element.150, f32[24,128,64]{1,2,0:T(8,128)S(1)} %fusion.33), kind=kCustom, calls=%fused_computation.3.clone.clone.1 | custom fusion | flops 196608 | bytes 2359392 | tf_op jit(solution)/shard_map/while/body/eval_jaxpr/scatter-add | solution.py:81
  133.3 11.4 %gather_fusion = bf16[3072,64]{1,0:T(8,128)(2,1)} fusion(bf16[5120,64]{1,0:T(8,128)(2,1)S(1)} %get-tuple-element.172, s32[3072]{0:T(1024)S(1)} %fusion.31), kind=kCustom, calls=%fused_computation.clone.clone.1 | custom fusion | bytes 798720 | tf_op jit(solution)/shard_map/while/body/eval_jaxpr/gather | solution.py:71
  144.8 2.0 fusion.32
  146.8 5.0 %scatter_fusion = f32[24,64,128]{2,1,0:T(8,128)} fusion(f32[24,64,128]{2,1,0:T(8,128)} %get-tuple-element.161, s32[24]{0:T(128)S(1)} %get-tuple-element.150, f32[24,64,128]{2,1,0:T(8,128)S(1)} %fusion.32), kind=kCustom, calls=%fused_computation.2.clone.clone.1 | custom fusion | flops 196608 | bytes 2359392 | tf_op jit(solution)/shard_map/while/body/eval_jaxpr/scatter-add | solution.py:81
  151.8 11.4 %gather_fusion.1 = bf16[3072,64]{1,0:T(8,128)(2,1)} fusion(bf16[5120,64]{1,0:T(8,128)(2,1)S(1)} %get-tuple-element.174, s32[3072]{0:T(1024)S(1)} %fusion.31), kind=kCustom, calls=%fused_computation.1.clone.clone.1 | custom fusion | bytes 798720 | tf_op jit(solution)/shard_map/while/body/eval_jaxpr/gather | solution.py:72
  163.3 2.0 fusion.33
  165.3 4.9 %scatter_fusion.1 = f32[24,128,64]{1,2,0:T(8,128)} fusion(f32[24,128,64]{1,2,0:T(8,128)} %get-tuple-element.162, s32[24]{0:T(128)S(1)} %get-tuple-element.150, f32[24,128,64]{1,2,0:T(8,128)S(1)} %fusion.33), kind=kCustom, calls=%fused_computation.3.clone.clone.1 | custom fusion | flops 196608 | bytes 2359392 | tf_op jit(solution)/shard_map/while/body/eval_jaxpr/scatter-add | solution.py:81
  170.2 11.4 %gather_fusion = bf16[3072,64]{1,0:T(8,128)(2,1)} fusion(bf16[5120,64]{1,0:T(8,128)(2,1)S(1)} %get-tuple-element.172, s32[3072]{0:T(1024)S(1)} %fusion.31), kind=kCustom, calls=%fused_computation.clone.clone.1 | custom fusion | bytes 798720 | tf_op jit(solution)/shard_map/while/body/eval_jaxpr/gather | solution.py:71
  181.6 2.0 fusion.32
  183.6 4.9 %scatter_fusion = f32[24,64,128]{2,1,0:T(8,128)} fusion(f32[24,64,128]{2,1,0:T(8,128)} %get-tuple-element.161, s32[24]{0:T(128)S(1)} %get-tuple-element.150, f32[24,64,128]{2,1,0:T(8,128)S(1)} %fusion.32), kind=kCustom, calls=%fused_computation.2.clone.clone.1 | custom fusion | flops 196608 | bytes 2359392 | tf_op jit(solution)/shard_map/while/body/eval_jaxpr/scatter-add | solution.py:81
  188.6 11.4 %gather_fusion.1 = bf16[3072,64]{1,0:T(8,128)(2,1)} fusion(bf16[5120,64]{1,0:T(8,128)(2,1)S(1)} %get-tuple-element.174, s32[3072]{0:T(1024)S(1)} %fusion.31), kind=kCustom, calls=%fused_computation.1.clone.clone.1 | custom fusion | bytes 798720 | tf_op jit(solution)/shard_map/while/body/eval_jaxpr/gather | solution.py:72
  200.1 2.0 fusion.33
  202.1 4.7 %scatter_fusion.1 = f32[24,128,64]{1,2,0:T(8,128)} fusion(f32[24,128,64]{1,2,0:T(8,128)} %get-tuple-element.162, s32[24]{0:T(128)S(1)} %get-tuple-element.150, f32[24,128,64]{1,2,0:T(8,128)S(1)} %fusion.33), kind=kCustom, calls=%fused_computation.3.clone.clone.1 | custom fusion | flops 196608 | bytes 2359392 | tf_op jit(solution)/shard_map/while/body/eval_jaxpr/scatter-add | solution.py:81
  206.8 11.4 %gather_fusion = bf16[3072,64]{1,0:T(8,128)(2,1)} fusion(bf16[5120,64]{1,0:T(8,128)(2,1)S(1)} %get-tuple-element.172, s32[3072]{0:T(1024)S(1)} %fusion.31), kind=kCustom, calls=%fused_computation.clone.clone.1 | custom fusion | bytes 798720 | tf_op jit(solution)/shard_map/while/body/eval_jaxpr/gather | solution.py:71
  218.3 2.0 fusion.32
  220.3 4.9 %scatter_fusion = f32[24,64,128]{2,1,0:T(8,128)} fusion(f32[24,64,128]{2,1,0:T(8,128)} %get-tuple-element.161, s32[24]{0:T(128)S(1)} %get-tuple-element.150, f32[24,64,128]{2,1,0:T(8,128)S(1)} %fusion.32), kind=kCustom, calls=%fused_computation.2.clone.clone.1 | custom fusion | flops 196608 | bytes 2359392 | tf_op jit(solution)/shard_map/while/body/eval_jaxpr/scatter-add | solution.py:81
  225.3 11.4 %gather_fusion.1 = bf16[3072,64]{1,0:T(8,128)(2,1)} fusion(bf16[5120,64]{1,0:T(8,128)(2,1)S(1)} %get-tuple-element.174, s32[3072]{0:T(1024)S(1)} %fusion.31), kind=kCustom, calls=%fused_computation.1.clone.clone.1 | custom fusion | bytes 798720 | tf_op jit(solution)/shard_map/while/body/eval_jaxpr/gather | solution.py:72
  236.7 2.0 fusion.33
  238.8 4.8 %scatter_fusion.1 = f32[24,128,64]{1,2,0:T(8,128)} fusion(f32[24,128,64]{1,2,0:T(8,128)} %get-tuple-element.162, s32[24]{0:T(128)S(1)} %get-tuple-element.150, f32[24,128,64]{1,2,0:T(8,128)S(1)} %fusion.33), kind=kCustom, calls=%fused_computation.3.clone.clone.1 | custom fusion | flops 196608 | bytes 2359392 | tf_op jit(solution)/shard_map/while/body/eval_jaxpr/scatter-add | solution.py:81
  243.6 11.4 %gather_fusion = bf16[3072,64]{1,0:T(8,128)(2,1)} fusion(bf16[5120,64]{1,0:T(8,128)(2,1)S(1)} %get-tuple-element.172, s32[3072]{0:T(1024)S(1)} %fusion.31), kind=kCustom, calls=%fused_computation.clone.clone.1 | custom fusion | bytes 798720 | tf_op jit(solution)/shard_map/while/body/eval_jaxpr/gather | solution.py:71
  255.0 2.0 fusion.32
  257.0 5.0 %scatter_fusion = f32[24,64,128]{2,1,0:T(8,128)} fusion(f32[24,64,128]{2,1,0:T(8,128)} %get-tuple-element.161, s32[24]{0:T(128)S(1)} %get-tuple-element.150, f32[24,64,128]{2,1,0:T(8,128)S(1)} %fusion.32), kind=kCustom, calls=%fused_computation.2.clone.clone.1 | custom fusion | flops 196608 | bytes 2359392 | tf_op jit(solution)/shard_map/while/body/eval_jaxpr/scatter-add | solution.py:81
  262.0 5.4 %copy.35 = f32[24,128,64]{0,2,1:T(8,128)} copy(f32[24,128,64]{1,2,0:T(8,128)} %get-tuple-element.49) | data formatting | bytes 1572864 | tf_op jit(solution)/shard_map/while | solution.py:89
  268.2 73.7 %reduce-scatter.5.cloned.1.call-done = f32[24,128,16]{0,2,1:T(8,128)} async-done(((f32[24,128,64]{0,2,1:T(8,128)}), f32[24,128,16]{0,2,1:T(8,128)}) %reduce-scatter.5.cloned.1.call-update) | async-done | bytes 196624 | tf_op jit(solution)/shard_map/reduce_scatter | solution.py:92
  341.8 1.3 copy.46
  343.2 0.8 reshape.180
  344.0 7.3 %all_to_all.53 = f32[2,1,24576]{2,1,0:T(1,128)S(1)} all-to-all(f32[2,1,24576]{2,1,0:T(1,128)S(1)} %reshape.180), channel_id=1, replica_groups=mesh['row'=4,'col'=2,'layer'=4] {'col'}, dimensions={0} | all-to-all | bytes 393216 | tf_op jit(solution)/shard_map/all_to_all | solution.py:102
  351.8 1.2 reduce
  353.8 1.5 reshape.182
  355.3 5.2 %all-to-all-start.4 = ((f32[16,1,3072]{2,1,0:T(1,128)}), f32[16,1,3072]{2,1,0:T(1,128)S(1)}, u32[]{:S(2)}, u32[]{:S(2)}) async-start(f32[16,1,3072]{2,1,0:T(1,128)} %reshape.182), calls=%async_computation.6 | async-start | bytes 393216 | tf_op jit(solution)/shard_map/all_to_all | solution.py:105
  360.5 9.1 %reduce-scatter.3.cloned.1.call-done = f32[24,16,128]{2,1,0:T(8,128)} async-done(((f32[24,64,128]{2,1,0:T(8,128)}), f32[24,16,128]{2,1,0:T(8,128)}) %reduce-scatter.3.cloned.1.call-update) | async-done | bytes 196624 | tf_op jit(solution)/shard_map/reduce_scatter | solution.py:91
  369.7 1.7 copy.34
  371.6 3.9 all-to-all-start.2
  375.5 1.1 reduce.1
  377.4 1.3 copy.37
  379.4 1.2 all-to-all-done.2
  380.9 39.2 %psum.7 = f32[24,24]{1,0:T(8,128)} all-reduce(f32[24,24]{1,0:T(8,128)S(1)} %convolution_bitcast_fusion), channel_id=1, replica_groups=mesh['row'=4,'col'=2,'layer'=4] {'row','col','layer'}, use_global_device_ids=true, to_apply=%region_10.11 | all-reduce | flops 576 | bytes 4608 | tf_op jit(solution)/shard_map/psum | solution.py:115
  (45 shorter events, 10.9 us)
Async XLA Ops:
  10.6 25.2 %all-to-all-start = ((s32[8,12,2]{1,2,0:T(2,128)}), s32[8,12,2]{1,2,0:T(2,128)S(1)}, u32[]{:S(2)}, u32[]{:S(2)}) async-start(s32[8,12,2]{1,2,0:T(2,128)} %copy.29), calls=%async_computation | async-start | bytes 16384 | tf_op jit(solution)/shard_map/all_to_all | solution.py:52
  35.8 6.2 %copy-start = (bf16[5120,64]{0,1:T(8,128)(2,1)S(1)}, bf16[5120,64]{0,1:T(8,128)(2,1)}, u32[]{:S(2)}) copy-start(bf16[5120,64]{0,1:T(8,128)(2,1)} %param.14) | copy-start | bytes 1966084
  35.8 6.9 %copy-start.1 = (bf16[5120,64]{0,1:T(8,128)(2,1)S(1)}, bf16[5120,64]{0,1:T(8,128)(2,1)}, u32[]{:S(2)}) copy-start(bf16[5120,64]{0,1:T(8,128)(2,1)} %param.15) | copy-start | bytes 1966084
  35.8 77.2 %all-to-all-start.1 = ((bf16[96,128,128]{2,1,0:T(8,128)(2,1)}), bf16[96,128,128]{2,1,0:T(8,128)(2,1)}, u32[]{:S(2)}, u32[]{:S(2)}) async-start(bf16[96,128,128]{2,1,0:T(8,128)(2,1)} %scatter_fusion.2), calls=%async_computation.1 | async-start | bytes 6291456 | tf_op jit(solution)/shard_map/all_to_all | solution.py:45
  41.9 299.9 %reduce-scatter.5.cloned.1.call-start = ((), (), s32[]{:S(2)}) async-start(), calls=%async_computation.8 | async-start | bytes 5242880 | tf_op jit(solution)/shard_map/reduce_scatter | solution.py:92
  267.4 102.3 %reduce-scatter.3.cloned.1.call-start = ((), (), s32[]{:S(2)}) async-start(), calls=%async_computation.7 | async-start | bytes 983040 | tf_op jit(solution)/shard_map/reduce_scatter | solution.py:91
  355.3 16.3 %all-to-all-start.4 = ((f32[16,1,3072]{2,1,0:T(1,128)}), f32[16,1,3072]{2,1,0:T(1,128)S(1)}, u32[]{:S(2)}, u32[]{:S(2)}) async-start(f32[16,1,3072]{2,1,0:T(1,128)} %reshape.182), calls=%async_computation.6 | async-start | bytes 393216 | tf_op jit(solution)/shard_map/all_to_all | solution.py:105
  371.6 9.0 %all-to-all-start.2 = ((f32[24,1,2,8,128]{4,0,3,1,2:T(8,128)}), f32[24,1,2,8,128]{4,0,3,1,2:T(8,128)S(1)}, u32[]{:S(2)}, u32[]{:S(2)}) async-start(f32[24,1,2,8,128]{4,0,3,1,2:T(8,128)} %bitcast.3), calls=%async_computation.3 | async-start | bytes 393216 | tf_op jit(solution)/shard_map/all_to_all | solution.py:101
Sparse Core Ops, SparseCore 0:
  267.5 74.2 reduce-scatter.4
  344.2 25.3 reduce-scatter.2
where the time goes:
time: 430 us; the launch traced here: 427 us
  waiting for transfers between devices  154 us (36%)
  local copies, waits for them, and re-layouts  127 us (30%)
  other arithmetic  46.9 us (11%)
  blocking collectives  46.5 us (11%)
  starting transfers between devices  22.5 us (5%)
  matrix products  16.5 us (4%)
  between operations  13.6 us (3%)
    reduce_scatter x1, waiting for transfers between devices, on_device(): lax.psum_scatter(virt_total, 'layer', scatter_dimension=2, tiled=True)  73.7 us
    all_to_all x1, waiting for transfers between devices, on_device(): lax.all_to_all(send_tiles.reshape(total_slots, tile_side, tile_side), ('c...  69.4 us
    gather x4, local copies, waits for them, and re-layouts, add_group(): virt_rows = virt_cols[row_index]  45.7 us
    gather x4, local copies, waits for them, and re-layouts, add_group(): occ_rows = occ_cols[row_index]  45.7 us
    psum x1, blocking collectives, on_device(): return lax.psum(chi_part, ('row', 'col', 'layer'))  39.2 us
    scatter-add x4, other arithmetic, add_group(): occ_total.at[aux_index].add(occ_term)  19.8 us
    scatter-add x4, other arithmetic, add_group(): virt_total.at[aux_index].add(virt_term)  19.2 us
    scatter x1, local copies, waits for them, and re-layouts, on_device(): send_tiles = jnp.zeros((owner_count * capacity, tile_side, tile_side), bl...  12.7 us
  transfers between devices with their start and end apart: 6, of which 5 were waited for; matrix products, arithmetic and copies ran while one was open for 7% of the time, Pallas kernels for 0%

commit v1 on v0

--- a/solution.py
+++ b/solution.py
@@ -1,9 +1,362 @@
 import jax
 import jax.numpy as jnp
 from jax import lax
+from jax.experimental import pallas as pl
+from jax.experimental.pallas import tpu as pltpu
 from jax.sharding import PartitionSpec as P
 
 NP = 24
+MESH = pl.DeviceIdType.MESH
+VMEM_LIMIT = 40 * 1024 * 1024
+OFFSETS = ((1, 2), (1, 1), (1, 3), (0, 2), (0, 1), (0, 3), (1, 0))
+
+
+def slot_kernel(cap, layers, layer_blocks, aux_ref, row_ref, col_ref, ext_ref, pick_ref, meta_ref, count):
+    held = aux_ref.shape[0]
+    owners = meta_ref.shape[0]
+
+    @pl.loop(0, owners)
+    def _(o):
+        count[o] = 0
+
+        @pl.loop(0, cap)
+        def _(j):
+            pick_ref[0, o * cap + j] = 0
+            pick_ref[1, o * cap + j] = 0
+            meta_ref[o, 0, j] = 0
+
+    @pl.loop(0, held)
+    def _(n):
+        block = col_ref[n]
+        layer = block // layer_blocks
+        owner = row_ref[n] * layers + layer
+        rank = count[owner]
+        count[owner] = rank + 1
+        pick_ref[0, owner * cap + rank] = n
+        pick_ref[1, owner * cap + rank] = ext_ref[n]
+        meta_ref[owner, 0, rank] = aux_ref[n] * 256 + block - layer * layer_blocks
+
+
+def place():
+    row, col, layer = lax.axis_index("row"), lax.axis_index("col"), lax.axis_index("layer")
+    return row // 2, row % 2, col, layer
+
+
+def exchange_kernel(cap, pick_ref, meta_ref, blocks_ref, occ_ref, virt_ref, tiles_ref, meta_out, green_ref,
+                    send_buf, green_in, meta_send, meta_recv, tile_send, tile_recv,
+                    y_send, y_recv, core_send, core_recv, green_send, green_recv):
+    y, core, col, layer = place()
+    row = 2 * y + core
+    across = 2 * (1 - y) + core
+    sibling = 2 * y + 1 - core
+    me = col * 4 + layer
+    part = cap // 4
+    side = blocks_ref.shape[1]
+
+    barrier = pltpu.get_barrier_semaphore()
+    peers = [(row, (col + dc) % 2, (layer + dl) % 4) for dc, dl in OFFSETS]
+    for peer in peers + [(across, col, layer), (sibling, col, layer)]:
+        pl.semaphore_signal(barrier, inc=1, device_id=peer, device_id_type=MESH)
+    pl.semaphore_wait(barrier, len(peers) + 2)
+
+    def greens(source):
+        return pltpu.make_async_remote_copy(
+            src_ref=source, dst_ref=green_in, send_sem=green_send, recv_sem=green_recv,
+            device_id=(sibling, col, layer), device_id_type=MESH)
+
+    @pl.when(core == 0)
+    def _():
+        greens(virt_ref).start()
+
+    @pl.when(core == 1)
+    def _():
+        greens(occ_ref).start()
+
+    lanes = lax.broadcasted_iota(jnp.int32, (side, side), 1)
+
+    def packed(owner, j):
+        slot = owner * cap + row * part + j
+        tile = blocks_ref[pick_ref[0, slot]]
+        return jnp.where(lanes < pick_ref[1, slot], tile.astype(jnp.float32), 0.0).astype(tile.dtype)
+
+    first = []
+    for k, peer in enumerate(peers):
+        owner = peer[1] * 4 + peer[2]
+        for j in range(part):
+            send_buf[k, j] = packed(owner, j)
+        tile_copy = pltpu.make_async_remote_copy(
+            src_ref=send_buf.at[k], dst_ref=tiles_ref.at[row, me], send_sem=tile_send.at[k],
+            recv_sem=tile_recv.at[k], device_id=peer, device_id_type=MESH)
+        tile_copy.start()
+        meta_copy = pltpu.make_async_remote_copy(
+            src_ref=meta_ref.at[owner], dst_ref=meta_out.at[me], send_sem=meta_send.at[k],
+            recv_sem=meta_recv.at[k], device_id=peer, device_id_type=MESH)
+        meta_copy.start()
+        first += [tile_copy, meta_copy]
+    for j in range(part):
+        tiles_ref[row, me, j] = packed(me, j)
+    meta_out[me] = meta_ref[me]
+
+    def forward(quarter, source, send, recv, k, target):
+        copy = pltpu.make_async_remote_copy(
+            src_ref=tiles_ref.at[quarter, source], dst_ref=tiles_ref.at[quarter, source],
+            send_sem=send.at[k], recv_sem=recv.at[k], device_id=(target, col, layer), device_id_type=MESH)
+        copy.start()
+        return copy
+
+    sources = [((col + dc) % 2) * 4 + (layer + 4 - dl) % 4 for dc, dl in OFFSETS] + [me]
+    order = [7, 6, 4, 5, 1, 2, 3, 0]
+    to_y, to_core = {}, {}
+    for k in order:
+        if k < 7:
+            first[2 * k].wait_recv()
+        to_y[k] = forward(row, sources[k], y_send, y_recv, k, across)
+        to_core[k] = forward(row, sources[k], core_send, core_recv, k, sibling)
+
+    greens(virt_ref).wait()
+    half = green_in.shape[1]
+
+    @pl.when(core == 0)
+    def _():
+        green_ref[:, :half] = occ_ref[...]
+        green_ref[:, half:] = green_in[...]
+
+    @pl.when(core == 1)
+    def _():
+        green_ref[:, :half] = green_in[...]
+        green_ref[:, half:] = virt_ref[...]
+
+    for k in order:
+        to_y[k].wait_recv()
+        to_core[8 + k] = forward(across, sources[k], core_send, core_recv, 8 + k, sibling)
+    for k in range(7):
+        first[2 * k].wait_send()
+        first[2 * k + 1].wait()
+    for k in order:
+        to_y[k].wait_send()
+        to_core[k].wait()
+        to_core[8 + k].wait()
+
+
+def product_kernel(cap, meta_ref, tiles_ref, green_ref, total_ref):
+    part = cap // 4
+    side = tiles_ref.shape[-1]
+    total_ref[...] = jnp.zeros_like(total_ref)
+
+    @pl.loop(0, tiles_ref.shape[0] * tiles_ref.shape[1] // 2)
+    def _(i):
+        terms = []
+        for h in range(2):
+            n = 2 * i + h
+            quarter, source = n // tiles_ref.shape[1], n % tiles_ref.shape[1]
+            for j in range(part):
+                code = meta_ref[source, 0, quarter * part + j]
+                start = pl.multiple_of((code % 256) * side, side)
+                terms.append((code // 256, jnp.dot(tiles_ref[quarter, source, j], green_ref[pl.ds(start, side), :],
+                                                   preferred_element_type=jnp.float32)))
+        for aux, term in terms:
+            total_ref[aux] += term
+
+    @pl.when(lax.axis_index("row") % 2 == 1)
+    def _():
+        @pl.loop(0, total_ref.shape[0])
+        def _(p):
+            total_ref[p] = total_ref[p].T
+
+
+def pair_kernel(total_ref, chi_ref, occ_in, virt_in, chi_buf, chi_in, send_sem, occ_sem, virt_sem,
+                chi_send, chi_recv):
+    y, core, x, z = place()
+    row = 2 * y + core
+    rows = occ_in.shape[2]
+    diagonal = x == y
+    partners = [
+        (2 * y + 1 - core, x, z), (2 * (1 - y) + core, x, z), (row, 1 - x, z),
+        (row, x, z + 1 - 2 * (z % 2)), (row, x, (z + 2) % 4)]
+
+    barrier = pltpu.get_barrier_semaphore()
+    for peer in partners[1:3]:
+        pl.semaphore_signal(barrier, inc=1, device_id=peer, device_id_type=MESH)
+    for dz in range(4):
+        for dk in range(2):
+            if dz or dk:
+                pl.semaphore_signal(barrier, inc=1, device_id=(2 * y + (core + dk) % 2, x, (z + dz) % 4),
+                                    device_id_type=MESH)
+    @pl.when(jnp.logical_not(diagonal))
+    def _():
+        for dz in range(4):
+            for dk in range(2):
+                pl.semaphore_signal(barrier, inc=1, device_id=(2 * x + (core + dk) % 2, y, (z + dz) % 4),
+                                    device_id_type=MESH)
+
+    pl.semaphore_wait(barrier, 9 + 8 * (x - y) * (x - y))
+
+    def part_of(kk, zz):
+        return total_ref.at[:, pl.ds(pl.multiple_of((2 * zz + kk) * rows, rows), rows), :]
+
+    def remote(into, sem, chip, kk, dz):
+        zz = (z + dz) % 4
+        return pltpu.make_async_remote_copy(
+            src_ref=part_of(kk, zz), dst_ref=into.at[dz], send_sem=send_sem.at[dz * 2 + kk], recv_sem=sem.at[dz],
+            device_id=(2 * chip[1] + kk, chip[0], zz), device_id_type=MESH)
+
+    def local(into, sem):
+        return pltpu.make_async_copy(part_of(core, z), into.at[0], sem.at[0])
+
+    here, there = (x, y), (y, x)
+    alone = jnp.logical_and(diagonal, core == 1)
+    far_first = (2, 1, 3, 0)
+
+    @pl.when(core == 0)
+    def _():
+        for dz in far_first:
+            for kk in (1, 0):
+                if dz == 0 and kk == 0:
+                    local(occ_in, occ_sem).start()
+                else:
+                    remote(occ_in, occ_sem, here, kk, dz).start()
+
+    @pl.when(core == 1)
+    def _():
+        for dz in far_first:
+            for kk in (0, 1):
+                if dz == 0 and kk == 1:
+                    @pl.when(diagonal)
+                    def _():
+                        local(virt_in, virt_sem).start()
+
+                    @pl.when(jnp.logical_not(diagonal))
+                    def _():
+                        remote(virt_in, virt_sem, there, kk, dz).start()
+                else:
+                    remote(virt_in, virt_sem, there, kk, dz).start()
+
+    for dz in (0, 1, 3, 2):
+        if dz:
+            remote(occ_in, occ_sem, here, 0, dz).wait_recv()
+            remote(virt_in, virt_sem, there, 1, dz).wait_recv()
+        else:
+            @pl.when(core == 0)
+            def _():
+                local(occ_in, occ_sem).wait()
+
+            @pl.when(core == 1)
+            def _():
+                remote(occ_in, occ_sem, here, 0, 0).wait_recv()
+
+            @pl.when(alone)
+            def _():
+                local(virt_in, virt_sem).wait()
+
+            @pl.when(jnp.logical_not(alone))
+            def _():
+                remote(virt_in, virt_sem, there, 1, 0).wait_recv()
+
+    occ_in[0] = (occ_in[0] + occ_in[1]) + (occ_in[2] + occ_in[3])
+    virt_in[0] = (virt_in[0] + virt_in[1]) + (virt_in[2] + virt_in[3])
+    count = total_ref.shape[0]
+    chi = jnp.zeros((count, count), jnp.float32)
+    for i in range(0, rows, 2):
+        left = jnp.concatenate([occ_in[0, :, i, :], occ_in[0, :, i + 1, :]], axis=1)
+        right = jnp.concatenate([virt_in[0, :, i, :], virt_in[0, :, i + 1, :]], axis=1)
+        chi += lax.dot_general(left, right, (((1,), (1,)), ((), ())), precision=lax.Precision.HIGHEST,
+                               preferred_element_type=jnp.float32)
+    chi_buf[...] = jnp.zeros_like(chi_buf)
+    chi_buf[0, :, :count] = chi
+
+    for k, partner in enumerate(partners):
+        copy = pltpu.make_async_remote_copy(
+            src_ref=chi_buf.at[k], dst_ref=chi_in.at[k], send_sem=chi_send.at[k], recv_sem=chi_recv.at[k],
+            device_id=partner, device_id_type=MESH)
+        copy.start()
+        copy.wait()
+        chi_buf[k + 1] = chi_buf[k] + chi_in[k]
+    chi_ref[...] = chi_buf[len(partners), :, :count]
+
+    @pl.when(core == 0)
+    def _():
+        for dz in far_first:
+            for kk in (1, 0):
+                if dz or kk:
+                    remote(occ_in, occ_sem, here, kk, dz).wait_send()
+
+    @pl.when(core == 1)
+    def _():
+        for dz in far_first:
+            remote(virt_in, virt_sem, there, 0, dz).wait_send()
+            if dz:
+                remote(virt_in, virt_sem, there, 1, dz).wait_send()
+
+        @pl.when(jnp.logical_not(diagonal))
+        def _():
+            remote(virt_in, virt_sem, there, 1, 0).wait_send()
+
+
+def on_slice(blocks, block_aux, block_row, block_col, extents, occ_green, virt_green):
+    held, side, _ = blocks.shape
+    layers, owners = 4, 8
+    cap = held // owners + 1
+    depth, width = occ_green.shape
+    smem, vmem = pl.BlockSpec(memory_space=pltpu.SMEM), pl.BlockSpec(memory_space=pltpu.VMEM)
+    f32, i32 = jnp.float32, jnp.int32
+    dma = pltpu.SemaphoreType.DMA
+
+    def bind(kernel, *sizes):
+        def run(*refs):
+            kernel(*sizes, *refs)
+        return run
+
+    pick, meta = pl.pallas_call(
+        bind(slot_kernel, cap, layers, depth // side),
+        out_shape=(jax.ShapeDtypeStruct((2, 128), i32), jax.ShapeDtypeStruct((owners, 8, 128), i32)),
+        in_specs=[smem] * 4,
+        out_specs=(smem, smem),
+        scratch_shapes=[pltpu.SMEM((owners,), i32)],
+        name="slots",
+    )(block_aux, block_row, block_col, extents)
+    part = cap // 4
+    tiles, meta, green = pl.pallas_call(
+        bind(exchange_kernel, cap),
+        out_shape=(
+            jax.ShapeDtypeStruct((4, owners, part, side, side), blocks.dtype),
+            jax.ShapeDtypeStruct((owners, 8, 128), i32),
+            jax.ShapeDtypeStruct((depth, 2 * width), occ_green.dtype),
+        ),
+        in_specs=[smem, vmem, vmem, vmem, vmem],
+        out_specs=(vmem, vmem, vmem),
+        scratch_shapes=[
+            pltpu.VMEM((7, part, side, side), blocks.dtype),
+            pltpu.VMEM((depth, width), occ_green.dtype),
+            dma((7,)), dma((7,)), dma((7,)), dma((7,)), dma((8,)), dma((8,)), dma((16,)), dma((16,)),
+            dma(()), dma(()),
+        ],
+        compiler_params=pltpu.CompilerParams(collective_id=0, has_side_effects=True, vmem_limit_bytes=VMEM_LIMIT),
+        name="exchange",
+    )(pick, meta, blocks, occ_green, virt_green)
+    total = pl.pallas_call(
+        bind(product_kernel, cap),
+        out_shape=jax.ShapeDtypeStruct((NP, side, 2 * width), f32),
+        in_specs=[smem, vmem, vmem],
+        out_specs=vmem,
+        compiler_params=pltpu.CompilerParams(vmem_limit_bytes=VMEM_LIMIT),
+        name="product",
+    )(meta, tiles, green)
+    thin = side // 8
+    return pl.pallas_call(
+        pair_kernel,
+        out_shape=jax.ShapeDtypeStruct((NP, NP), f32),
+        in_specs=[vmem],
+        out_specs=vmem,
+        scratch_shapes=[
+            pltpu.VMEM((4, NP, thin, side), f32),
+            pltpu.VMEM((4, NP, thin, side), f32),
+            pltpu.VMEM((6, NP, 128), f32),
+            pltpu.VMEM((5, NP, 128), f32),
+            dma((8,)), dma((4,)), dma((4,)), dma((5,)), dma((5,)),
+        ],
+        compiler_params=pltpu.CompilerParams(collective_id=1, has_side_effects=True, vmem_limit_bytes=VMEM_LIMIT),
+        name="pair",
+    )(total)
 
 
 def on_device(blocks, block_aux, block_row, block_col, extents, occ_green, virt_green):
@@ -126,6 +479,7 @@
         P("layer", "row"),
     )
     out_specs = P()
+    side_of = (mesh.shape["row"], mesh.shape["col"], mesh.shape["layer"])
     return jax.shard_map(
-        on_device, mesh=mesh, in_specs=in_specs, out_specs=out_specs, check_vma=False
-    )
+        on_slice if side_of == (4, 2, 4) else on_device, mesh=mesh, in_specs=in_specs, out_specs=out_specs, check_vma=False
+    )

time: 430 us -> 106 us (0.25)
  waiting for transfers between devices: 154 us -> 0 us
  local copies, waits for them, and re-layouts: 127 us -> 4.83 us
  Pallas kernels: 0 us -> 101 us
  other arithmetic: 46.9 us -> 0 us
  blocking collectives: 46.5 us -> 0 us
  starting transfers between devices: 22.5 us -> 0 us
  matrix products: 16.5 us -> 0 us
  between operations: 13.6 us -> 0.1 us
    pallas_call x0 -> x4, Pallas kernels: none -> 101 us  [the longest x1 55.7 us: on_slice(): pl.pallas_call(pair_kernel, out_shape=jax.ShapeDtypeStruct((NP, NP), f32)...]
    gather x8 -> x0, local copies, waits for them, and re-layouts: 91.5 us -> none  [the longest x4 45.7 us: add_group(): virt_rows = virt_cols[row_index]]
    reduce_scatter x2 -> x0, waiting for transfers between devices: 82.8 us -> none  [the longest x1 73.7 us: on_device(): lax.psum_scatter(virt_total, 'layer', scatter_dimension=2, tiled=True)]
    all_to_all x4 -> x0, waiting for transfers between devices: 70.9 us -> none  [the longest x1 69.4 us: on_device(): lax.all_to_all(send_tiles.reshape(total_slots, tile_side, tile_side), ('c...]
    psum x1 -> x0, blocking collectives: 39.2 us -> none  [on_device(): return lax.psum(chi_part, ('row', 'col', 'layer'))]
    scatter-add x8 -> x0, other arithmetic: 39 us -> none  [the longest x4 19.8 us: add_group(): occ_total.at[aux_index].add(occ_term)]
    all_to_all x4 -> x0, starting transfers between devices: 22.4 us -> none  [the longest x1 7.25 us: on_device(): lax.all_to_all(send_meta.reshape(total_slots, 2), ('col', 'layer'), split...]
    dot_general x9 -> x0, matrix products: 16.5 us -> none  [the longest x4 8.08 us: add_group(): jnp.einsum('gvs,gsl->gvl', tile_group, virt_rows, preferred_element_type=...]
  transfers between devices with their start and end apart: 6 -> 0, of which waited for: 5 -> 0; matrix products, arithmetic and copies ran while one was open for 7% -> 0% of each run, Pallas kernels for 0% -> 0%
where the time goes in v1:
time: 106 us
  Pallas kernels  101 us (95%)
  local copies, waits for them, and re-layouts  4.83 us (5%)
    pallas_call x1, Pallas kernels, on_slice(): pl.pallas_call(pair_kernel, out_shape=jax.ShapeDtypeStruct((NP, NP), f32)...  55.7 us
    pallas_call x1, Pallas kernels, on_slice(): pl.pallas_call(bind(exchange_kernel, cap), out_shape=(jax.ShapeDtypeStruc...  35.1 us
    pallas_call x1, Pallas kernels, on_slice(): pl.pallas_call(bind(slot_kernel, cap, layers, depth // side), out_shape=(...  5.27 us
    unnamed x11, local copies, waits for them, and re-layouts  4.83 us
    pallas_call x1, Pallas kernels, on_slice(): pl.pallas_call(bind(product_kernel, cap), out_shape=jax.ShapeDtypeStruct(...  4.77 us

profile of v1, /device:TPU:0, one launch (start us, length us, event | category | flops | bytes accessed | tf_op | source)
XLA Modules:
  0.0 105.7 jit_solution(9012908861355749134)
XLA Ops:
  0.0 0.0 copy-start.3
  0.0 5.3 %slots.1 = (s32[2,128]{1,0:T(2,128)}, s32[8,8,128]{2,1,0:T(8,128)}) custom-call(s32[88]{0:T(128)} %refs_0_.1, s32[88]{0:T(128)} %refs_1_.1, s32[88]{0:T(128)} %refs_2_.2, s32[88]{0:T(128)} %refs_3_.2), custom_call_target="tpu_custom_call" | custom-call | tf_op jit(solution)/shard_map/slots/pallas_call | solution.py:309
  5.3 0.0 copy-start.1
  5.3 0.0 copy-start.2
  5.3 1.7 %copy.8.refs_3_ = bf16[5120,64]{1,0:T(8,128)(2,1)S(1)} copy(bf16[5120,64]{0,1:T(8,128)(2,1)} %param.12) | data formatting | bytes 1310720 | tf_op args[5]
  7.0 0.0 copy-done.3
  7.0 0.7 copy.9.refs_4_
  7.7 0.0 copy-done.1
  7.7 0.0 copy-done.2
  7.8 0.0 copy-start
  7.8 1.8 %copy-done = bf16[88,128,128]{2,1,0:T(8,128)(2,1)S(1)} copy-done((bf16[88,128,128]{2,1,0:T(8,128)(2,1)S(1)}, bf16[88,128,128]{2,1,0:T(8,128)(2,1)}, u32[]{:S(2)}) %copy-start) | copy-done | bytes 2883608
  9.6 35.1 %exchange.1 = (bf16[4,8,3,128,128]{4,3,2,1,0:T(8,128)(2,1)S(1)}, s32[8,8,128]{2,1,0:T(8,128)S(1)}, bf16[5120,128]{1,0:T(8,128)(2,1)S(1)}) custom-call(s32[2,128]{1,0:T(2,128)S(1)} %copy-done.2, s32[8,8,128]{2,1,0:T(8,128)S(1)} %copy-done.1, bf16[88,128,128]{2,1,0:T(8,128)(2,1)S(1)} %copy-done, bf16[5120,64]{1,0:T(8,128)(2,1)S(1)} %copy.8.refs_3_, ...), custom_call_target="tpu_custom_call" | custom-call | tf_op jit(solution)/shard_map/exchange/pallas_call | solution.py:318
  44.6 4.8 %product.1.total_ref = f32[24,128,128]{2,1,0:T(8,128)S(1)} custom-call(s32[8,8,128]{2,1,0:T(8,128)S(1)} %get-tuple-element.12.refs_0_, bf16[4,8,3,128,128]{4,3,2,1,0:T(8,128)(2,1)S(1)} %get-tuple-element.13.refs_1_, bf16[5120,128]{1,0:T(8,128)(2,1)S(1)} %get-tuple-element.14.refs_2_), custom_call_target="tpu_custom_call" | custom-call | tf_op jit(solution)/shard_map/product/pallas_call | solution.py:336
  49.4 55.7 %pair.1 = f32[24,24]{1,0:T(8,128)S(1)} custom-call(f32[24,128,128]{2,1,0:T(8,128)S(1)} %product.1.total_ref), custom_call_target="tpu_custom_call" | custom-call | tf_op jit(solution)/shard_map/pair/pallas_call | solution.py:345
  105.1 0.6 copy.11
Async XLA Ops:
  0.0 7.0 %copy-start.3 = (bf16[5120,64]{0,1:T(8,128)(2,1)S(1)}, bf16[5120,64]{0,1:T(8,128)(2,1)}, u32[]{:S(2)}) copy-start(bf16[5120,64]{0,1:T(8,128)(2,1)} %param.13) | copy-start | bytes 1966084
  5.3 2.5 %copy-start.1 = (s32[8,8,128]{2,1,0:T(8,128)S(1)}, s32[8,8,128]{2,1,0:T(8,128)}, u32[]{:S(2)}) copy-start(s32[8,8,128]{2,1,0:T(8,128)} %get-tuple-element.11.refs_1_) | copy-start | bytes 98308
  5.3 2.5 %copy-start.2 = (s32[2,128]{1,0:T(2,128)S(1)}, s32[2,128]{1,0:T(2,128)}, u32[]{:S(2)}) copy-start(s32[2,128]{1,0:T(2,128)} %get-tuple-element.10.refs_0_) | copy-start | bytes 3076
  7.8 1.8 %copy-start = (bf16[88,128,128]{2,1,0:T(8,128)(2,1)S(1)}, bf16[88,128,128]{2,1,0:T(8,128)(2,1)}, u32[]{:S(2)}) copy-start(bf16[88,128,128]{2,1,0:T(8,128)(2,1)} %refs_2_.3) | copy-start | bytes 8650756

commit v2 on v0

--- a/solution.py
+++ b/solution.py
@@ -1,9 +1,431 @@
 import jax
 import jax.numpy as jnp
 from jax import lax
+from jax.experimental import pallas as pl
+from jax.experimental.pallas import tpu as pltpu
 from jax.sharding import PartitionSpec as P
 
 NP = 24
+MESH = pl.DeviceIdType.MESH
+VMEM_LIMIT = 40 * 1024 * 1024
+STEPS = 8
+OFFSETS = ((1, 2), (1, 1), (1, 3), (0, 2), (0, 1), (0, 3), (1, 0))
+
+
+def slot_kernel(cap, layers, layer_blocks, aux_ref, row_ref, col_ref, ext_ref, pick_ref, meta_ref):
+    held = aux_ref.shape[0]
+    owners = meta_ref.shape[0]
+    for o in range(owners):
+        for j in range(cap):
+            pick_ref[o * cap + j] = 0
+            meta_ref[o, 0, j] = 0
+
+    def put(n, counts):
+        block = col_ref[n]
+        layer = jnp.int32(0)
+        for edge in range(1, layers):
+            layer += (block >= edge * layer_blocks).astype(jnp.int32)
+        owner = row_ref[n] * layers + layer
+        rank = lax.shift_right_logical(counts, 4 * owner) & 15
+        pick_ref[owner * cap + rank] = n * 256 + ext_ref[n]
+        meta_ref[owner, 0, rank] = aux_ref[n] * 256 + block - layer * layer_blocks
+        return counts + lax.shift_left(jnp.int32(1), 4 * owner)
+
+    lax.fori_loop(0, held, put, jnp.int32(0), unroll=8)
+
+
+def place():
+    row, col, layer = lax.axis_index("row"), lax.axis_index("col"), lax.axis_index("layer")
+    return row // 2, row % 2, col, layer
+
+
+def exchange_kernel(cap, pick_ref, meta_ref, blocks_ref, occ_ref, virt_ref, tiles_ref, meta_out, green_ref,
+                    send_buf, meta_send, meta_recv, tile_send, tile_recv,
+                    y_send, y_recv, core_send, core_recv, green_send, green_recv):
+    y, core, col, layer = place()
+    row = 2 * y + core
+    across = 2 * (1 - y) + core
+    sibling = 2 * y + 1 - core
+    me = col * 4 + layer
+    part = cap // 4
+    side = blocks_ref.shape[1]
+
+    barrier = pltpu.get_barrier_semaphore()
+    peers = [(row, (col + dc) % 2, (layer + dl) % 4) for dc, dl in OFFSETS]
+    for peer in peers + [(across, col, layer), (sibling, col, layer)]:
+        pl.semaphore_signal(barrier, inc=1, device_id=peer, device_id_type=MESH)
+    pl.semaphore_wait(barrier, len(peers) + 2)
+
+    half = occ_ref.shape[0]
+    own_rows = pl.ds(pl.multiple_of(core * half, half), half)
+
+    def greens(source):
+        return pltpu.make_async_remote_copy(
+            src_ref=source, dst_ref=green_ref.at[own_rows], send_sem=green_send, recv_sem=green_recv,
+            device_id=(sibling, col, layer), device_id_type=MESH)
+
+    @pl.when(core == 0)
+    def _():
+        greens(virt_ref).start()
+        green_ref[:half] = occ_ref[...]
+
+    @pl.when(core == 1)
+    def _():
+        greens(occ_ref).start()
+        green_ref[half:] = virt_ref[...]
+
+    lanes = lax.broadcasted_iota(jnp.int32, (side, side), 1)
+
+    def packed(owner, j):
+        pick = pick_ref[owner * cap + row * part + j]
+        tile = blocks_ref[pick // 256]
+        return jnp.where(lanes < pick % 256, tile.astype(jnp.float32), 0.0).astype(tile.dtype)
+
+    def forward(quarter, source, send, recv, k, target):
+        copy = pltpu.make_async_remote_copy(
+            src_ref=tiles_ref.at[quarter, source], dst_ref=tiles_ref.at[quarter, source],
+            send_sem=send.at[k], recv_sem=recv.at[k], device_id=(target, col, layer), device_id_type=MESH)
+        copy.start()
+        return copy
+
+    sources = [((col + dc) % 2) * 4 + (layer + 4 - dl) % 4 for dc, dl in OFFSETS] + [me]
+    order = [7, 6, 4, 5, 1, 2, 3, 0]
+    to_y, to_core = {}, {}
+    for j in range(part):
+        tiles_ref[row, me, j] = packed(me, j)
+    to_y[7] = forward(row, me, y_send, y_recv, 7, across)
+    to_core[7] = forward(row, me, core_send, core_recv, 7, sibling)
+    meta_out[me] = meta_ref[me]
+    first = []
+    for k, peer in enumerate(peers):
+        owner = peer[1] * 4 + peer[2]
+        for j in range(part):
+            send_buf[k, j] = packed(owner, j)
+        tile_copy = pltpu.make_async_remote_copy(
+            src_ref=send_buf.at[k], dst_ref=tiles_ref.at[row, me], send_sem=tile_send.at[k],
+            recv_sem=tile_recv.at[k], device_id=peer, device_id_type=MESH)
+        tile_copy.start()
+        meta_copy = pltpu.make_async_remote_copy(
+            src_ref=meta_ref.at[owner], dst_ref=meta_out.at[me], send_sem=meta_send.at[k],
+            recv_sem=meta_recv.at[k], device_id=peer, device_id_type=MESH)
+        meta_copy.start()
+        first += [tile_copy, meta_copy]
+
+    for k in order:
+        if k == 7:
+            continue
+        first[2 * k].wait_recv()
+        to_y[k] = forward(row, sources[k], y_send, y_recv, k, across)
+        to_core[k] = forward(row, sources[k], core_send, core_recv, k, sibling)
+
+    greens(virt_ref).wait()
+    for k in order:
+        to_y[k].wait_recv()
+        to_core[8 + k] = forward(across, sources[k], core_send, core_recv, 8 + k, sibling)
+    for k in range(7):
+        first[2 * k].wait_send()
+        first[2 * k + 1].wait()
+    for k in order:
+        to_y[k].wait_send()
+        to_core[k].wait()
+        to_core[8 + k].wait()
+
+
+def product_kernel(cap, meta_ref, tiles_ref, green_ref, total_ref):
+    part = cap // 4
+    side = tiles_ref.shape[-1]
+    total_ref[...] = jnp.zeros_like(total_ref)
+
+    def add_all(flipped):
+        @pl.loop(0, tiles_ref.shape[0] * tiles_ref.shape[1] // 2)
+        def _(i):
+            terms = []
+            for h in range(2):
+                n = 2 * i + h
+                quarter, source = n // tiles_ref.shape[1], n % tiles_ref.shape[1]
+                for j in range(part):
+                    code = meta_ref[source, 0, quarter * part + j]
+                    start = pl.multiple_of((code % 256) * side, side)
+                    pair = (tiles_ref[quarter, source, j], green_ref[:, pl.ds(start, side)])
+                    terms.append((code // 256, lax.dot_general(
+                        *(pair[::-1] if flipped else pair), (((1,), (1,)), ((), ())),
+                        preferred_element_type=jnp.float32)))
+            for aux, term in terms:
+                total_ref[aux] += term
+
+    core = lax.axis_index("row") % 2
+    pl.when(core == 0)(lambda: add_all(False))
+    pl.when(core == 1)(lambda: add_all(True))
+
+
+def pair_kernel(total_ref, chi_ref, right_in, left_in, done, occ_in, virt_in, plane_in, line_in,
+                right_send, right_recv, left_send, left_recv, occ_send, occ_recv, virt_send, virt_recv,
+                plane_send, plane_recv, line_send, line_recv):
+    y, core, x, z = place()
+    row = 2 * y + core
+    count = total_ref.shape[0]
+    rows = right_in.shape[1]
+    thin = rows // 2
+    steps = STEPS
+    size = count // steps
+    diagonal = x == y
+    end = jnp.logical_or(z == 0, z == 3)
+
+    def device(number):
+        return (2 * (number // 4) + number % 2, (number // 2) % 2, z)
+
+    mine = 4 * y + 2 * x + core
+    barrier = pltpu.get_barrier_semaphore()
+    for k in range(1, 4):
+        pl.semaphore_signal(barrier, inc=1, device_id=(row, x, (z + k) % 4), device_id_type=MESH)
+    for k in range(1, 8):
+        pl.semaphore_signal(barrier, inc=1, device_id=device((mine + k) % 8), device_id_type=MESH)
+    pl.semaphore_wait(barrier, 10)
+
+    def chunk(c):
+        return pl.ds(c * size, size)
+
+    def right(c, source):
+        return pltpu.make_async_remote_copy(
+            src_ref=source, dst_ref=right_in.at[chunk(c)], send_sem=right_send.at[c], recv_sem=right_recv.at[c],
+            device_id=(row, x, (z + 1) % 4), device_id_type=MESH)
+
+    def left(c, source):
+        return pltpu.make_async_remote_copy(
+            src_ref=source, dst_ref=left_in.at[chunk(c)], send_sem=left_send.at[c], recv_sem=left_recv.at[c],
+            device_id=(row, x, (z + 3) % 4), device_id_type=MESH)
+
+    def pass_right(c):
+        right(c, right_in.at[chunk(c)]).wait_recv()
+        right_in[chunk(c)] += total_ref[chunk(c), rows:]
+        right(c, right_in.at[chunk(c)]).start()
+
+    def pass_left(c):
+        left(c, left_in.at[chunk(c)]).wait_recv()
+        left_in[chunk(c)] += total_ref[chunk(c), :rows]
+        left(c, left_in.at[chunk(c)]).start()
+
+    def occ_copy(c):
+        return pltpu.make_async_remote_copy(
+            src_ref=done.at[chunk(c), thin:], dst_ref=occ_in.at[chunk(c)], send_sem=occ_send.at[c],
+            recv_sem=occ_recv.at[c], device_id=(2 * y + 1 - core, x, z), device_id_type=MESH)
+
+    def virt_copy(c, kk):
+        return pltpu.make_async_remote_copy(
+            src_ref=done.at[chunk(c), kk * thin:(kk + 1) * thin], dst_ref=virt_in.at[chunk(c)],
+            send_sem=virt_send.at[c, kk], recv_sem=virt_recv.at[c], device_id=(2 * x + kk, y, z),
+            device_id_type=MESH)
+
+    def hand_out(c):
+        @pl.when(core == 0)
+        def _():
+            occ_copy(c).start()
+            occ_in[chunk(c)] = done[chunk(c), :thin]
+
+        @pl.when(core == 1)
+        def _():
+            virt_copy(c, 0).start()
+
+            @pl.when(diagonal)
+            def _():
+                virt_in[chunk(c)] = done[chunk(c), thin:]
+
+            @pl.when(jnp.logical_not(diagonal))
+            def _():
+                virt_copy(c, 1).start()
+
+    lag = 2
+
+    @pl.when(z == 0)
+    def _():
+        for c in range(steps + lag):
+            if c < steps:
+                if c >= 3:
+                    right(c - 3, total_ref.at[chunk(c - 3), rows:]).wait_send()
+                right(c, total_ref.at[chunk(c), rows:]).start()
+            if c >= lag:
+                e = c - lag
+                left(e, left_in.at[chunk(e)]).wait_recv()
+                done[chunk(e)] = left_in[chunk(e)] + total_ref[chunk(e), :rows]
+                hand_out(e)
+        for c in range(steps - 3, steps):
+            right(c, total_ref.at[chunk(c), rows:]).wait_send()
+
+    @pl.when(z == 3)
+    def _():
+        for c in range(steps + lag):
+            if c < steps:
+                if c >= 3:
+                    left(c - 3, total_ref.at[chunk(c - 3), :rows]).wait_send()
+                left(c, total_ref.at[chunk(c), :rows]).start()
+            if c >= lag:
+                e = c - lag
+                right(e, right_in.at[chunk(e)]).wait_recv()
+                done[chunk(e)] = right_in[chunk(e)] + total_ref[chunk(e), rows:]
+                hand_out(e)
+        for c in range(steps - 3, steps):
+            left(c, total_ref.at[chunk(c), :rows]).wait_send()
+
+    def relay(near, far):
+        for c in range(steps + 1):
+            if c < steps:
+                near(c)
+            if c >= 1:
+                far(c - 1)
+
+    pl.when(z == 1)(lambda: relay(pass_right, pass_left))
+    pl.when(z == 2)(lambda: relay(pass_left, pass_right))
+
+    @pl.when(jnp.logical_not(end))
+    def _():
+        for c in range(steps):
+            right(c, right_in.at[chunk(c)]).wait_send()
+            left(c, left_in.at[chunk(c)]).wait_send()
+
+    def plane(k):
+        return pltpu.make_async_remote_copy(
+            src_ref=plane_in.at[mine], dst_ref=plane_in.at[mine], send_sem=plane_send.at[k],
+            recv_sem=plane_recv.at[k], device_id=device((mine + k) % 8), device_id_type=MESH)
+
+    def line(which, k):
+        return pltpu.make_async_remote_copy(
+            src_ref=line_in.at[which], dst_ref=line_in.at[which], send_sem=line_send.at[k],
+            recv_sem=line_recv.at[which], device_id=(row, x, (z + k) % 4), device_id_type=MESH)
+
+    @pl.when(end)
+    def _():
+        for c in range(steps):
+            @pl.when(core == 1)
+            def _():
+                occ_copy(c).wait_recv()
+
+            @pl.when(jnp.logical_not(jnp.logical_and(diagonal, core == 1)))
+            def _():
+                virt_copy(c, 0).wait_recv()
+        chi = jnp.zeros((count, count), jnp.float32)
+        for i in range(0, thin, 2):
+            first = jnp.concatenate([occ_in[:, i, :], occ_in[:, i + 1, :]], axis=1)
+            second = jnp.concatenate([virt_in[:, i, :], virt_in[:, i + 1, :]], axis=1)
+            chi += lax.dot_general(first, second, (((1,), (1,)), ((), ())), precision=lax.Precision.HIGHEST,
+                                   preferred_element_type=jnp.float32)
+        plane_in[mine] = jnp.pad(chi, ((0, 0), (0, 128 - count)))
+        for k in range(1, 8):
+            plane(k).start()
+        for k in range(1, 8):
+            plane(k).wait_recv()
+        summed = plane_in[0]
+        for k in range(1, 8):
+            summed += plane_in[k]
+
+        @pl.when(z == 0)
+        def _():
+            line_in[0] = summed
+            for k in (3, 2, 1):
+                line(0, k).start()
+
+        @pl.when(z == 3)
+        def _():
+            line_in[1] = summed
+            for k in (1, 2, 3):
+                line(1, k).start()
+
+    @pl.when(z > 0)
+    def _():
+        line(0, 1).wait_recv()
+
+    @pl.when(z < 3)
+    def _():
+        line(1, 1).wait_recv()
+
+    chi_ref[...] = (line_in[0] + line_in[1])[:, :count]
+
+    @pl.when(end)
+    def _():
+        for k in range(1, 8):
+            plane(k).wait_send()
+        for k in range(1, 4):
+            line(0, k).wait_send()
+        for c in range(steps):
+            @pl.when(core == 0)
+            def _():
+                occ_copy(c).wait_send()
+
+            @pl.when(core == 1)
+            def _():
+                virt_copy(c, 0).wait_send()
+
+                @pl.when(jnp.logical_not(diagonal))
+                def _():
+                    virt_copy(c, 1).wait_send()
+
+
+def on_slice(blocks, block_aux, block_row, block_col, extents, occ_green, virt_green):
+    held, side, _ = blocks.shape
+    layers, owners = 4, 8
+    cap = held // owners + 1
+    depth, width = occ_green.shape
+    smem, vmem = pl.BlockSpec(memory_space=pltpu.SMEM), pl.BlockSpec(memory_space=pltpu.VMEM)
+    f32, i32 = jnp.float32, jnp.int32
+    dma = pltpu.SemaphoreType.DMA
+
+    def bind(kernel, *sizes):
+        def run(*refs):
+            kernel(*sizes, *refs)
+        return run
+
+    pick, meta = pl.pallas_call(
+        bind(slot_kernel, cap, layers, depth // side),
+        out_shape=(jax.ShapeDtypeStruct((128,), i32), jax.ShapeDtypeStruct((owners, 8, 128), i32)),
+        in_specs=[smem] * 4,
+        out_specs=(smem, smem),
+        name="slots",
+    )(block_aux, block_row, block_col, extents)
+    part = cap // 4
+    tiles, meta, green = pl.pallas_call(
+        bind(exchange_kernel, cap),
+        out_shape=(
+            jax.ShapeDtypeStruct((4, owners, part, side, side), blocks.dtype),
+            jax.ShapeDtypeStruct((owners, 8, 128), i32),
+            jax.ShapeDtypeStruct((2 * width, depth), occ_green.dtype),
+        ),
+        in_specs=[smem, vmem, vmem, vmem, vmem],
+        out_specs=(vmem, vmem, vmem),
+        scratch_shapes=[
+            pltpu.VMEM((7, part, side, side), blocks.dtype),
+            dma((7,)), dma((7,)), dma((7,)), dma((7,)), dma((8,)), dma((8,)), dma((16,)), dma((16,)),
+            dma(()), dma(()),
+        ],
+        compiler_params=pltpu.CompilerParams(collective_id=0, has_side_effects=True, vmem_limit_bytes=VMEM_LIMIT),
+        name="exchange",
+    )(pick, meta, blocks, occ_green.T, virt_green.T)
+    total = pl.pallas_call(
+        bind(product_kernel, cap),
+        out_shape=jax.ShapeDtypeStruct((NP, side, 2 * width), f32),
+        in_specs=[smem, vmem, vmem],
+        out_specs=vmem,
+        compiler_params=pltpu.CompilerParams(vmem_limit_bytes=VMEM_LIMIT),
+        name="product",
+    )(meta, tiles, green)
+    rows, part_rows = side // 2, side // 4
+    return pl.pallas_call(
+        pair_kernel,
+        out_shape=jax.ShapeDtypeStruct((NP, NP), f32),
+        in_specs=[vmem],
+        out_specs=vmem,
+        scratch_shapes=[
+            pltpu.VMEM((NP, rows, side), f32),
+            pltpu.VMEM((NP, rows, side), f32),
+            pltpu.VMEM((NP, rows, side), f32),
+            pltpu.VMEM((NP, part_rows, side), f32),
+            pltpu.VMEM((NP, part_rows, side), f32),
+            pltpu.VMEM((8, NP, 128), f32),
+            pltpu.VMEM((2, NP, 128), f32),
+            dma((STEPS,)), dma((STEPS,)), dma((STEPS,)), dma((STEPS,)), dma((STEPS,)), dma((STEPS,)),
+            dma((STEPS, 2)), dma((STEPS,)), dma((8,)), dma((8,)), dma((4,)), dma((2,)),
+        ],
+        compiler_params=pltpu.CompilerParams(collective_id=1, has_side_effects=True, vmem_limit_bytes=VMEM_LIMIT),
+        name="pair",
+    )(total)
 
 
 def on_device(blocks, block_aux, block_row, block_col, extents, occ_green, virt_green):
@@ -126,6 +548,7 @@
         P("layer", "row"),
     )
     out_specs = P()
+    side_of = (mesh.shape["row"], mesh.shape["col"], mesh.shape["layer"])
     return jax.shard_map(
-        on_device, mesh=mesh, in_specs=in_specs, out_specs=out_specs, check_vma=False
-    )
+        on_slice if side_of == (4, 2, 4) else on_device, mesh=mesh, in_specs=in_specs, out_specs=out_specs, check_vma=False
+    )

time: 430 us -> 105 us (0.24)
  waiting for transfers between devices: 154 us -> 0 us
  local copies, waits for them, and re-layouts: 127 us -> 6 us
  Pallas kernels: 0 us -> 98.7 us
  other arithmetic: 46.9 us -> 0 us
  blocking collectives: 46.5 us -> 0 us
  starting transfers between devices: 22.5 us -> 0 us
  matrix products: 16.5 us -> 0 us
  between operations: 13.6 us -> 0.05 us
    pallas_call x0 -> x4, Pallas kernels: none -> 98.7 us  [the longest x1 55 us: on_slice(): pl.pallas_call(pair_kernel, out_shape=jax.ShapeDtypeStruct((NP, NP), f32)...]
    gather x8 -> x0, local copies, waits for them, and re-layouts: 91.5 us -> none  [the longest x4 45.7 us: add_group(): virt_rows = virt_cols[row_index]]
    reduce_scatter x2 -> x0, waiting for transfers between devices: 82.8 us -> none  [the longest x1 73.7 us: on_device(): lax.psum_scatter(virt_total, 'layer', scatter_dimension=2, tiled=True)]
    all_to_all x4 -> x0, waiting for transfers between devices: 70.9 us -> none  [the longest x1 69.4 us: on_device(): lax.all_to_all(send_tiles.reshape(total_slots, tile_side, tile_side), ('c...]
    psum x1 -> x0, blocking collectives: 39.2 us -> none  [on_device(): return lax.psum(chi_part, ('row', 'col', 'layer'))]
    scatter-add x8 -> x0, other arithmetic: 39 us -> none  [the longest x4 19.8 us: add_group(): occ_total.at[aux_index].add(occ_term)]
    all_to_all x4 -> x0, starting transfers between devices: 22.4 us -> none  [the longest x1 7.25 us: on_device(): lax.all_to_all(send_meta.reshape(total_slots, 2), ('col', 'layer'), split...]
    dot_general x9 -> x0, matrix products: 16.5 us -> none  [the longest x4 8.08 us: add_group(): jnp.einsum('gvs,gsl->gvl', tile_group, virt_rows, preferred_element_type=...]
  transfers between devices with their start and end apart: 6 -> 0, of which waited for: 5 -> 0; matrix products, arithmetic and copies ran while one was open for 7% -> 0% of each run, Pallas kernels for 0% -> 0%
where the time goes in v2:
time: 105 us
  Pallas kernels  98.7 us (94%)
  local copies, waits for them, and re-layouts  6 us (6%)
    pallas_call x1, Pallas kernels, on_slice(): pl.pallas_call(pair_kernel, out_shape=jax.ShapeDtypeStruct((NP, NP), f32)...  55 us
    pallas_call x1, Pallas kernels, on_slice(): pl.pallas_call(bind(exchange_kernel, cap), out_shape=(jax.ShapeDtypeStruc...  35.1 us
    unnamed x11, local copies, waits for them, and re-layouts  6 us
    pallas_call x1, Pallas kernels, on_slice(): pl.pallas_call(bind(product_kernel, cap), out_shape=jax.ShapeDtypeStruct(...  5.63 us
    pallas_call x1, Pallas kernels, on_slice(): pl.pallas_call(bind(slot_kernel, cap, layers, depth // side), out_shape=(...  2.95 us

profile of v2, /device:TPU:0, one launch (start us, length us, event | category | flops | bytes accessed | tf_op | source)
XLA Modules:
  0.0 104.8 jit_solution(13070342207935127268)
XLA Ops:
  0.0 2.9 %slots.1 = (s32[128]{0:T(128)}, s32[8,8,128]{2,1,0:T(8,128)}) custom-call(s32[88]{0:T(128)} %refs_0_.1, s32[88]{0:T(128)} %refs_1_.1, s32[88]{0:T(128)} %refs_2_.2, s32[88]{0:T(128)} %refs_3_.1), custom_call_target="tpu_custom_call" | custom-call | tf_op jit(solution)/shard_map/slots/pallas_call | solution.py:376
  3.0 0.0 copy-start
  3.0 1.8 %copy-done = bf16[88,128,128]{2,1,0:T(8,128)(2,1)S(1)} copy-done((bf16[88,128,128]{2,1,0:T(8,128)(2,1)S(1)}, bf16[88,128,128]{2,1,0:T(8,128)(2,1)}, u32[]{:S(2)}) %copy-start) | copy-done | bytes 2883608
  4.8 0.0 copy-start.1
  4.8 1.1 %copy-done.1 = bf16[5120,64]{0,1:T(8,128)(2,1)S(1)} copy-done((bf16[5120,64]{0,1:T(8,128)(2,1)S(1)}, bf16[5120,64]{0,1:T(8,128)(2,1)}, u32[]{:S(2)}) %copy-start.1) | copy-done | bytes 655384
  5.9 0.0 copy-start.2
  5.9 1.1 %copy-done.2 = bf16[5120,64]{0,1:T(8,128)(2,1)S(1)} copy-done((bf16[5120,64]{0,1:T(8,128)(2,1)S(1)}, bf16[5120,64]{0,1:T(8,128)(2,1)}, u32[]{:S(2)}) %copy-start.2) | copy-done | bytes 655384
  6.9 0.0 copy-start.3
  7.0 0.8 copy-done.3
  7.7 0.0 copy-start.4
  7.7 0.7 copy-done.4
  8.4 35.1 %exchange.1 = (bf16[4,8,3,128,128]{4,3,2,1,0:T(8,128)(2,1)S(1)}, s32[8,8,128]{2,1,0:T(8,128)S(1)}, bf16[128,5120]{1,0:T(8,128)(2,1)S(1)}) custom-call(s32[128]{0:T(128)S(1)} %copy-done.4, s32[8,8,128]{2,1,0:T(8,128)S(1)} %copy-done.3, bf16[88,128,128]{2,1,0:T(8,128)(2,1)S(1)} %copy-done, bf16[64,5120]{1,0:T(8,128)(2,1)S(1)} %bitcast.2, ...), custom_call_target="tpu_custom_call" | custom-call | tf_op jit(solution)/shard_map/exchange/pallas_call | solution.py:384
  43.5 5.6 %product.1.total_ref = f32[24,128,128]{2,1,0:T(8,128)S(1)} custom-call(s32[8,8,128]{2,1,0:T(8,128)S(1)} %get-tuple-element.12.refs_0_, bf16[4,8,3,128,128]{4,3,2,1,0:T(8,128)(2,1)S(1)} %get-tuple-element.13.refs_1_, bf16[128,5120]{1,0:T(8,128)(2,1)S(1)} %get-tuple-element.14.refs_2_), custom_call_target="tpu_custom_call" | custom-call | tf_op jit(solution)/shard_map/product/pallas_call | solution.py:401
  49.1 55.0 %pair.1 = f32[24,24]{1,0:T(8,128)S(1)} custom-call(f32[24,128,128]{2,1,0:T(8,128)S(1)} %product.1.total_ref), custom_call_target="tpu_custom_call" | custom-call | tf_op jit(solution)/shard_map/pair/pallas_call | solution.py:410
  104.2 0.6 copy.9
Async XLA Ops:
  3.0 1.8 %copy-start = (bf16[88,128,128]{2,1,0:T(8,128)(2,1)S(1)}, bf16[88,128,128]{2,1,0:T(8,128)(2,1)}, u32[]{:S(2)}) copy-start(bf16[88,128,128]{2,1,0:T(8,128)(2,1)} %refs_2_.3) | copy-start | bytes 8650756
  4.8 1.1 %copy-start.1 = (bf16[5120,64]{0,1:T(8,128)(2,1)S(1)}, bf16[5120,64]{0,1:T(8,128)(2,1)}, u32[]{:S(2)}) copy-start(bf16[5120,64]{0,1:T(8,128)(2,1)} %param.12) | copy-start | bytes 1966084
  5.9 1.1 %copy-start.2 = (bf16[5120,64]{0,1:T(8,128)(2,1)S(1)}, bf16[5120,64]{0,1:T(8,128)(2,1)}, u32[]{:S(2)}) copy-start(bf16[5120,64]{0,1:T(8,128)(2,1)} %param.13) | copy-start | bytes 1966084
  6.9 0.8 copy-start.3
  7.7 0.7 copy-start.4

commit v3 on v2

--- a/solution.py
+++ b/solution.py
@@ -9,16 +9,16 @@
 MESH = pl.DeviceIdType.MESH
 VMEM_LIMIT = 40 * 1024 * 1024
 STEPS = 8
-OFFSETS = ((1, 2), (1, 1), (1, 3), (0, 2), (0, 1), (0, 3), (1, 0))
-
-
-def slot_kernel(cap, layers, layer_blocks, aux_ref, row_ref, col_ref, ext_ref, pick_ref, meta_ref):
+OFFSETS = ((0, 3), (1, 0), (1, 2), (0, 1), (1, 3), (0, 2), (1, 1))
+
+
+def slot_kernel(cap, layers, layer_blocks, aux_ref, row_ref, col_ref, ext_ref, code_ref):
     held = aux_ref.shape[0]
-    owners = meta_ref.shape[0]
+    owners = code_ref.shape[1]
     for o in range(owners):
         for j in range(cap):
-            pick_ref[o * cap + j] = 0
-            meta_ref[o, 0, j] = 0
+            code_ref[0, o, 0, j] = 0
+            code_ref[1, o, 0, j] = 0
 
     def put(n, counts):
         block = col_ref[n]
@@ -27,8 +27,8 @@
             layer += (block >= edge * layer_blocks).astype(jnp.int32)
         owner = row_ref[n] * layers + layer
         rank = lax.shift_right_logical(counts, 4 * owner) & 15
-        pick_ref[owner * cap + rank] = n * 256 + ext_ref[n]
-        meta_ref[owner, 0, rank] = aux_ref[n] * 256 + block - layer * layer_blocks
+        code_ref[0, owner, 0, rank] = n * 256 + ext_ref[n]
+        code_ref[1, owner, 0, rank] = aux_ref[n] * 256 + block - layer * layer_blocks
         return counts + lax.shift_left(jnp.int32(1), 4 * owner)
 
     lax.fori_loop(0, held, put, jnp.int32(0), unroll=8)
@@ -39,8 +39,8 @@
     return row // 2, row % 2, col, layer
 
 
-def exchange_kernel(cap, pick_ref, meta_ref, blocks_ref, occ_ref, virt_ref, tiles_ref, meta_out, green_ref,
-                    send_buf, meta_send, meta_recv, tile_send, tile_recv,
+def exchange_kernel(cap, code_ref, blocks_hbm, occ_hbm, virt_hbm, tiles_ref, meta_out, green_ref,
+                    blocks_ref, own_green, codes, meta_ref, send_buf, load_sem, meta_send, meta_recv, tile_send, tile_recv,
                     y_send, y_recv, core_send, core_recv, green_send, green_recv):
     y, core, col, layer = place()
     row = 2 * y + core
@@ -49,37 +49,62 @@
     me = col * 4 + layer
     part = cap // 4
     side = blocks_ref.shape[1]
-
+    half = own_green.shape[0]
+    own_rows = pl.ds(pl.multiple_of(core * half, half), half)
+
+    load_codes = pltpu.make_async_copy(code_ref.at[0], codes, load_sem.at[0])
+    load_meta = pltpu.make_async_copy(code_ref.at[1], meta_ref, load_sem.at[1])
+    load_blocks = pltpu.make_async_copy(blocks_hbm, blocks_ref, load_sem.at[2])
+    load_codes.start()
+    load_meta.start()
+    load_blocks.start()
+
+    def load_own(source):
+        return pltpu.make_async_copy(source, green_ref.at[own_rows], load_sem.at[3])
+
+    def load_other(source):
+        return pltpu.make_async_copy(source, own_green, load_sem.at[4])
+
+    @pl.when(core == 0)
+    def _():
+        load_other(virt_hbm).start()
+        load_own(occ_hbm).start()
+
+    @pl.when(core == 1)
+    def _():
+        load_other(occ_hbm).start()
+        load_own(virt_hbm).start()
+
+    layers_by = (layer, layer + 1 - 2 * (layer % 2), (layer + 2) % 4, 3 - layer)
     barrier = pltpu.get_barrier_semaphore()
-    peers = [(row, (col + dc) % 2, (layer + dl) % 4) for dc, dl in OFFSETS]
+    peers = [(row, 1 - col if dc else col, layers_by[dl]) for dc, dl in OFFSETS]
     for peer in peers + [(across, col, layer), (sibling, col, layer)]:
         pl.semaphore_signal(barrier, inc=1, device_id=peer, device_id_type=MESH)
     pl.semaphore_wait(barrier, len(peers) + 2)
 
-    half = occ_ref.shape[0]
-    own_rows = pl.ds(pl.multiple_of(core * half, half), half)
-
-    def greens(source):
-        return pltpu.make_async_remote_copy(
-            src_ref=source, dst_ref=green_ref.at[own_rows], send_sem=green_send, recv_sem=green_recv,
-            device_id=(sibling, col, layer), device_id_type=MESH)
-
-    @pl.when(core == 0)
-    def _():
-        greens(virt_ref).start()
-        green_ref[:half] = occ_ref[...]
-
-    @pl.when(core == 1)
-    def _():
-        greens(occ_ref).start()
-        green_ref[half:] = virt_ref[...]
-
+    greens = pltpu.make_async_remote_copy(
+        src_ref=own_green, dst_ref=green_ref.at[own_rows], send_sem=green_send, recv_sem=green_recv,
+        device_id=(sibling, col, layer), device_id_type=MESH)
     lanes = lax.broadcasted_iota(jnp.int32, (side, side), 1)
 
     def packed(owner, j):
-        pick = pick_ref[owner * cap + row * part + j]
+        pick = codes[owner, 0, row * part + j]
         tile = blocks_ref[pick // 256]
         return jnp.where(lanes < pick % 256, tile.astype(jnp.float32), 0.0).astype(tile.dtype)
+
+    def owner_of(peer):
+        return peer[1] * 4 + peer[2]
+
+    def pack(k):
+        for j in range(part):
+            send_buf[k, j] = packed(owner_of(peers[k]), j)
+
+    tile_copies = [pltpu.make_async_remote_copy(
+        src_ref=send_buf.at[k], dst_ref=tiles_ref.at[row, me], send_sem=tile_send.at[k],
+        recv_sem=tile_recv.at[k], device_id=peer, device_id_type=MESH) for k, peer in enumerate(peers)]
+    meta_copies = [pltpu.make_async_remote_copy(
+        src_ref=meta_ref.at[owner_of(peer)], dst_ref=meta_out.at[me], send_sem=meta_send.at[k],
+        recv_sem=meta_recv.at[k], device_id=peer, device_id_type=MESH) for k, peer in enumerate(peers)]
 
     def forward(quarter, source, send, recv, k, target):
         copy = pltpu.make_async_remote_copy(
@@ -88,43 +113,54 @@
         copy.start()
         return copy
 
-    sources = [((col + dc) % 2) * 4 + (layer + 4 - dl) % 4 for dc, dl in OFFSETS] + [me]
-    order = [7, 6, 4, 5, 1, 2, 3, 0]
+    sources = [owner_of(peer) for peer in peers] + [me]
+    order = [7] + list(range(7))
     to_y, to_core = {}, {}
+    window = 3
+    load_codes.wait()
+    load_blocks.wait()
+
+    def send(k):
+        pack(k)
+        tile_copies[k].start()
+
+    send(0)
     for j in range(part):
         tiles_ref[row, me, j] = packed(me, j)
     to_y[7] = forward(row, me, y_send, y_recv, 7, across)
     to_core[7] = forward(row, me, core_send, core_recv, 7, sibling)
+    for k in range(1, window):
+        send(k)
+    load_other(virt_hbm).wait()
+    greens.start()
+    load_meta.wait()
+    for copy in meta_copies:
+        copy.start()
     meta_out[me] = meta_ref[me]
-    first = []
-    for k, peer in enumerate(peers):
-        owner = peer[1] * 4 + peer[2]
-        for j in range(part):
-            send_buf[k, j] = packed(owner, j)
-        tile_copy = pltpu.make_async_remote_copy(
-            src_ref=send_buf.at[k], dst_ref=tiles_ref.at[row, me], send_sem=tile_send.at[k],
-            recv_sem=tile_recv.at[k], device_id=peer, device_id_type=MESH)
-        tile_copy.start()
-        meta_copy = pltpu.make_async_remote_copy(
-            src_ref=meta_ref.at[owner], dst_ref=meta_out.at[me], send_sem=meta_send.at[k],
-            recv_sem=meta_recv.at[k], device_id=peer, device_id_type=MESH)
-        meta_copy.start()
-        first += [tile_copy, meta_copy]
-
-    for k in order:
-        if k == 7:
-            continue
-        first[2 * k].wait_recv()
+
+    for k in range(window, 7):
+        pack(k)
+    for k in range(7):
+        if k + window < 7:
+            tile_copies[k].wait_send()
+            tile_copies[k + window].start()
+        tile_copies[k].wait_recv()
         to_y[k] = forward(row, sources[k], y_send, y_recv, k, across)
         to_core[k] = forward(row, sources[k], core_send, core_recv, k, sibling)
-
-    greens(virt_ref).wait()
-    for k in order:
-        to_y[k].wait_recv()
-        to_core[8 + k] = forward(across, sources[k], core_send, core_recv, 8 + k, sibling)
+        if k >= 1:
+            e = order[k - 1]
+            to_y[e].wait_recv()
+            to_core[8 + e] = forward(across, sources[e], core_send, core_recv, 8 + e, sibling)
+
+    for e in order[6:]:
+        to_y[e].wait_recv()
+        to_core[8 + e] = forward(across, sources[e], core_send, core_recv, 8 + e, sibling)
+    load_own(occ_hbm).wait()
+    greens.wait()
     for k in range(7):
-        first[2 * k].wait_send()
-        first[2 * k + 1].wait()
+        if k + window >= 7:
+            tile_copies[k].wait_send()
+        meta_copies[k].wait()
     for k in order:
         to_y[k].wait_send()
         to_core[k].wait()
@@ -234,7 +270,7 @@
             def _():
                 virt_copy(c, 1).start()
 
-    lag = 2
+    lag = 6
 
     @pl.when(z == 0)
     def _():
@@ -267,11 +303,11 @@
             left(c, total_ref.at[chunk(c), :rows]).wait_send()
 
     def relay(near, far):
-        for c in range(steps + 1):
+        for c in range(steps + 2):
             if c < steps:
                 near(c)
-            if c >= 1:
-                far(c - 1)
+            if c >= 2:
+                far(c - 2)
 
     pl.when(z == 1)(lambda: relay(pass_right, pass_left))
     pl.when(z == 2)(lambda: relay(pass_left, pass_right))
@@ -373,11 +409,11 @@
             kernel(*sizes, *refs)
         return run
 
-    pick, meta = pl.pallas_call(
+    codes = pl.pallas_call(
         bind(slot_kernel, cap, layers, depth // side),
-        out_shape=(jax.ShapeDtypeStruct((128,), i32), jax.ShapeDtypeStruct((owners, 8, 128), i32)),
+        out_shape=jax.ShapeDtypeStruct((2, owners, 8, 128), i32),
         in_specs=[smem] * 4,
-        out_specs=(smem, smem),
+        out_specs=smem,
         name="slots",
     )(block_aux, block_row, block_col, extents)
     part = cap // 4
@@ -388,16 +424,21 @@
             jax.ShapeDtypeStruct((owners, 8, 128), i32),
             jax.ShapeDtypeStruct((2 * width, depth), occ_green.dtype),
         ),
-        in_specs=[smem, vmem, vmem, vmem, vmem],
+        in_specs=[pl.BlockSpec(memory_space=pl.ANY)] * 4,
         out_specs=(vmem, vmem, vmem),
         scratch_shapes=[
+            pltpu.VMEM(blocks.shape, blocks.dtype),
+            pltpu.VMEM((width, depth), occ_green.dtype),
+            pltpu.SMEM((owners, 8, 128), i32),
+            pltpu.VMEM((owners, 8, 128), i32),
             pltpu.VMEM((7, part, side, side), blocks.dtype),
+            dma((5,)),
             dma((7,)), dma((7,)), dma((7,)), dma((7,)), dma((8,)), dma((8,)), dma((16,)), dma((16,)),
             dma(()), dma(()),
         ],
         compiler_params=pltpu.CompilerParams(collective_id=0, has_side_effects=True, vmem_limit_bytes=VMEM_LIMIT),
         name="exchange",
-    )(pick, meta, blocks, occ_green.T, virt_green.T)
+    )(codes, blocks, occ_green.T, virt_green.T)
     total = pl.pallas_call(
         bind(product_kernel, cap),
         out_shape=jax.ShapeDtypeStruct((NP, side, 2 * width), f32),

time: 105 us -> 89.7 us (0.85)
  Pallas kernels: 98.7 us -> 84 us
    pallas_call x1, Pallas kernels: 55 us -> 40.2 us  [on_slice(): pl.pallas_call(pair_kernel, out_shape=jax.ShapeDtypeStruct((NP, NP), f32)...]
    unnamed x11 -> x9, local copies, waits for them, and re-layouts: 6 us -> 5.42 us
where the time goes in v3:
time: 89.7 us; the launch traced here: 89.5 us
  Pallas kernels  84 us (94%)
  local copies, waits for them, and re-layouts  5.42 us (6%)
    pallas_call x1, Pallas kernels, on_slice(): pl.pallas_call(pair_kernel, out_shape=jax.ShapeDtypeStruct((NP, NP), f32)...  40.2 us
    pallas_call x1, Pallas kernels, on_slice(): pl.pallas_call(bind(exchange_kernel, cap), out_shape=(jax.ShapeDtypeStruc...  34.8 us
    pallas_call x1, Pallas kernels, on_slice(): pl.pallas_call(bind(product_kernel, cap), out_shape=jax.ShapeDtypeStruct(...  5.63 us
    unnamed x9, local copies, waits for them, and re-layouts  5.42 us
    pallas_call x1, Pallas kernels, on_slice(): pl.pallas_call(bind(slot_kernel, cap, layers, depth // side), out_shape=j...  3.35 us

profile of v3, /device:TPU:0, one launch (start us, length us, event | category | flops | bytes accessed | tf_op | source)
XLA Modules:
  0.0 89.5 jit_solution(5490531863095718801)
XLA Ops:
  0.0 3.3 %slots.1.refs_0_ = s32[2,8,8,128]{3,2,1,0:T(8,128)} custom-call(s32[88]{0:T(128)} %refs_0_.1, s32[88]{0:T(128)} %refs_1_.2, s32[88]{0:T(128)} %refs_2_.1, s32[88]{0:T(128)} %refs_3_.1), custom_call_target="tpu_custom_call" | custom-call | tf_op jit(solution)/shard_map/slots/pallas_call | solution.py:412
  3.4 0.0 copy-start
  3.4 1.8 %copy-done = bf16[88,128,128]{2,1,0:T(8,128)(2,1)S(1)} copy-done((bf16[88,128,128]{2,1,0:T(8,128)(2,1)S(1)}, bf16[88,128,128]{2,1,0:T(8,128)(2,1)}, u32[]{:S(2)}) %copy-start) | copy-done | bytes 2883608
  5.2 0.0 copy-start.1
  5.2 1.1 %copy-done.1 = bf16[5120,64]{0,1:T(8,128)(2,1)S(1)} copy-done((bf16[5120,64]{0,1:T(8,128)(2,1)S(1)}, bf16[5120,64]{0,1:T(8,128)(2,1)}, u32[]{:S(2)}) %copy-start.1) | copy-done | bytes 655384
  6.3 0.0 copy-start.2
  6.3 1.1 %copy-done.2 = bf16[5120,64]{0,1:T(8,128)(2,1)S(1)} copy-done((bf16[5120,64]{0,1:T(8,128)(2,1)S(1)}, bf16[5120,64]{0,1:T(8,128)(2,1)}, u32[]{:S(2)}) %copy-start.2) | copy-done | bytes 655384
  7.4 0.0 copy-start.3
  7.4 0.8 copy-done.3
  8.2 34.8 %exchange.1 = (bf16[4,8,3,128,128]{4,3,2,1,0:T(8,128)(2,1)S(1)}, s32[8,8,128]{2,1,0:T(8,128)S(1)}, bf16[128,5120]{1,0:T(8,128)(2,1)S(1)}) custom-call(s32[2,8,8,128]{3,2,1,0:T(8,128)S(1)} %copy-done.3, bf16[88,128,128]{2,1,0:T(8,128)(2,1)S(1)} %copy-done, bf16[64,5120]{1,0:T(8,128)(2,1)S(1)} %bitcast.2, bf16[64,5120]{1,0:T(8,128)(2,1)S(1)} %bitcast.3), custom_call_target="tpu_custom_call" | custom-call | tf_op jit(solution)/shard_map/exchange/pallas_call | solution.py:420
  43.0 5.6 %product.1.total_ref = f32[24,128,128]{2,1,0:T(8,128)S(1)} custom-call(s32[8,8,128]{2,1,0:T(8,128)S(1)} %get-tuple-element.8.refs_0_, bf16[4,8,3,128,128]{4,3,2,1,0:T(8,128)(2,1)S(1)} %get-tuple-element.9.refs_1_, bf16[128,5120]{1,0:T(8,128)(2,1)S(1)} %get-tuple-element.10.refs_2_), custom_call_target="tpu_custom_call" | custom-call | tf_op jit(solution)/shard_map/product/pallas_call | solution.py:442
  48.6 40.2 %pair.1 = f32[24,24]{1,0:T(8,128)S(1)} custom-call(f32[24,128,128]{2,1,0:T(8,128)S(1)} %product.1.total_ref), custom_call_target="tpu_custom_call" | custom-call | tf_op jit(solution)/shard_map/pair/pallas_call | solution.py:451
  88.9 0.6 copy.9
Async XLA Ops:
  3.4 1.8 %copy-start = (bf16[88,128,128]{2,1,0:T(8,128)(2,1)S(1)}, bf16[88,128,128]{2,1,0:T(8,128)(2,1)}, u32[]{:S(2)}) copy-start(bf16[88,128,128]{2,1,0:T(8,128)(2,1)} %refs_1_.3) | copy-start | bytes 8650756
  5.2 1.1 %copy-start.1 = (bf16[5120,64]{0,1:T(8,128)(2,1)S(1)}, bf16[5120,64]{0,1:T(8,128)(2,1)}, u32[]{:S(2)}) copy-start(bf16[5120,64]{0,1:T(8,128)(2,1)} %param.12) | copy-start | bytes 1966084
  6.3 1.1 %copy-start.2 = (bf16[5120,64]{0,1:T(8,128)(2,1)S(1)}, bf16[5120,64]{0,1:T(8,128)(2,1)}, u32[]{:S(2)}) copy-start(bf16[5120,64]{0,1:T(8,128)(2,1)} %param.13) | copy-start | bytes 1966084
  7.4 0.8 copy-start.3

commit v4 on v3

--- a/solution.py
+++ b/solution.py
@@ -9,29 +9,7 @@
 MESH = pl.DeviceIdType.MESH
 VMEM_LIMIT = 40 * 1024 * 1024
 STEPS = 8
-OFFSETS = ((0, 3), (1, 0), (1, 2), (0, 1), (1, 3), (0, 2), (1, 1))
-
-
-def slot_kernel(cap, layers, layer_blocks, aux_ref, row_ref, col_ref, ext_ref, code_ref):
-    held = aux_ref.shape[0]
-    owners = code_ref.shape[1]
-    for o in range(owners):
-        for j in range(cap):
-            code_ref[0, o, 0, j] = 0
-            code_ref[1, o, 0, j] = 0
-
-    def put(n, counts):
-        block = col_ref[n]
-        layer = jnp.int32(0)
-        for edge in range(1, layers):
-            layer += (block >= edge * layer_blocks).astype(jnp.int32)
-        owner = row_ref[n] * layers + layer
-        rank = lax.shift_right_logical(counts, 4 * owner) & 15
-        code_ref[0, owner, 0, rank] = n * 256 + ext_ref[n]
-        code_ref[1, owner, 0, rank] = aux_ref[n] * 256 + block - layer * layer_blocks
-        return counts + lax.shift_left(jnp.int32(1), 4 * owner)
-
-    lax.fori_loop(0, held, put, jnp.int32(0), unroll=8)
+OFFSETS = ((1, 0), (0, 3), (0, 1), (1, 2), (1, 1), (1, 3), (0, 2))
 
 
 def place():
@@ -39,8 +17,8 @@
     return row // 2, row % 2, col, layer
 
 
-def exchange_kernel(cap, code_ref, blocks_hbm, occ_hbm, virt_hbm, tiles_ref, meta_out, green_ref,
-                    blocks_ref, own_green, codes, meta_ref, send_buf, load_sem, meta_send, meta_recv, tile_send, tile_recv,
+def exchange_kernel(cap, layer_blocks, list_hbm, blocks_hbm, occ_hbm, virt_hbm, tiles_ref, meta_out, green_ref,
+                    blocks_ref, own_green, list_ref, code_ref, codes, meta_ref, send_buf, load_sem, meta_send, meta_recv, tile_send, tile_recv,
                     y_send, y_recv, core_send, core_recv, green_send, green_recv):
     y, core, col, layer = place()
     row = 2 * y + core
@@ -52,11 +30,10 @@
     half = own_green.shape[0]
     own_rows = pl.ds(pl.multiple_of(core * half, half), half)
 
-    load_codes = pltpu.make_async_copy(code_ref.at[0], codes, load_sem.at[0])
-    load_meta = pltpu.make_async_copy(code_ref.at[1], meta_ref, load_sem.at[1])
+    load_list = pltpu.make_async_copy(list_hbm, list_ref, load_sem.at[0])
+    load_codes = pltpu.make_async_copy(code_ref, codes, load_sem.at[1])
     load_blocks = pltpu.make_async_copy(blocks_hbm, blocks_ref, load_sem.at[2])
-    load_codes.start()
-    load_meta.start()
+    load_list.start()
     load_blocks.start()
 
     def load_own(source):
@@ -80,6 +57,30 @@
     peers = [(row, 1 - col if dc else col, layers_by[dl]) for dc, dl in OFFSETS]
     for peer in peers + [(across, col, layer), (sibling, col, layer)]:
         pl.semaphore_signal(barrier, inc=1, device_id=peer, device_id_type=MESH)
+    load_list.wait()
+    aux_list, row_list, col_list, ext_list = (list_ref[i:i + 1, :] for i in range(4))
+    layer_list = sum((col_list >= edge * layer_blocks).astype(jnp.int32) for edge in range(1, 4))
+    square = (8, 128)
+    lane = lax.broadcasted_iota(jnp.int32, square, 1)
+    owned = jnp.broadcast_to(row_list * 4 + layer_list, square) == lax.broadcasted_iota(jnp.int32, square, 0)
+    rank = owned.astype(jnp.int32)
+    step = 1
+    while step < 128:
+        rank += jnp.where(lane >= step, pltpu.roll(rank, step, 1), 0)
+        step *= 2
+    tile_code = lane * 256 + jnp.broadcast_to(ext_list, square)
+    meta_code = jnp.broadcast_to(aux_list * 256 + col_list - layer_list * layer_blocks, square)
+    tile_slots = jnp.zeros(square, jnp.int32)
+    meta_slots = jnp.zeros(square, jnp.int32)
+    for j in range(cap):
+        here = jnp.logical_and(owned, rank == j + 1)
+        tile_slots += jnp.where(lane == j, jnp.sum(jnp.where(here, tile_code, 0), axis=1, keepdims=True), 0)
+        meta_slots += jnp.where(lane == j, jnp.sum(jnp.where(here, meta_code, 0), axis=1, keepdims=True), 0)
+    code_ref[...] = tile_slots
+    load_codes.start()
+    for o in range(8):
+        meta_ref[o] = jnp.broadcast_to(meta_slots[o:o + 1, :], square)
+
     pl.semaphore_wait(barrier, len(peers) + 2)
 
     greens = pltpu.make_async_remote_copy(
@@ -88,7 +89,7 @@
     lanes = lax.broadcasted_iota(jnp.int32, (side, side), 1)
 
     def packed(owner, j):
-        pick = codes[owner, 0, row * part + j]
+        pick = codes[owner, row * part + j]
         tile = blocks_ref[pick // 256]
         return jnp.where(lanes < pick % 256, tile.astype(jnp.float32), 0.0).astype(tile.dtype)
 
@@ -116,7 +117,7 @@
     sources = [owner_of(peer) for peer in peers] + [me]
     order = [7] + list(range(7))
     to_y, to_core = {}, {}
-    window = 3
+    window = 4
     load_codes.wait()
     load_blocks.wait()
 
@@ -133,7 +134,6 @@
         send(k)
     load_other(virt_hbm).wait()
     greens.start()
-    load_meta.wait()
     for copy in meta_copies:
         copy.start()
     meta_out[me] = meta_ref[me]
@@ -338,12 +338,17 @@
             @pl.when(jnp.logical_not(jnp.logical_and(diagonal, core == 1)))
             def _():
                 virt_copy(c, 0).wait_recv()
-        chi = jnp.zeros((count, count), jnp.float32)
+        def halves(ref, i):
+            values = jnp.concatenate([ref[:, i, :], ref[:, i + 1, :]], axis=1)
+            high = values.astype(jnp.bfloat16)
+            low = (values - high.astype(jnp.float32)).astype(jnp.bfloat16)
+            return jnp.concatenate([high.astype(jnp.float32), low.astype(jnp.float32)], axis=0).astype(jnp.bfloat16)
+
+        both = jnp.zeros((2 * count, 2 * count), jnp.float32)
         for i in range(0, thin, 2):
-            first = jnp.concatenate([occ_in[:, i, :], occ_in[:, i + 1, :]], axis=1)
-            second = jnp.concatenate([virt_in[:, i, :], virt_in[:, i + 1, :]], axis=1)
-            chi += lax.dot_general(first, second, (((1,), (1,)), ((), ())), precision=lax.Precision.HIGHEST,
-                                   preferred_element_type=jnp.float32)
+            both += lax.dot_general(halves(occ_in, i), halves(virt_in, i), (((1,), (1,)), ((), ())),
+                                    preferred_element_type=jnp.float32)
+        chi = (both[:count, :count] + both[count:, count:]) + (both[:count, count:] + both[count:, :count])
         plane_in[mine] = jnp.pad(chi, ((0, 0), (0, 128 - count)))
         for k in range(1, 8):
             plane(k).start()
@@ -397,7 +402,7 @@
 
 def on_slice(blocks, block_aux, block_row, block_col, extents, occ_green, virt_green):
     held, side, _ = blocks.shape
-    layers, owners = 4, 8
+    owners = 8
     cap = held // owners + 1
     depth, width = occ_green.shape
     smem, vmem = pl.BlockSpec(memory_space=pltpu.SMEM), pl.BlockSpec(memory_space=pltpu.VMEM)
@@ -409,16 +414,11 @@
             kernel(*sizes, *refs)
         return run
 
-    codes = pl.pallas_call(
-        bind(slot_kernel, cap, layers, depth // side),
-        out_shape=jax.ShapeDtypeStruct((2, owners, 8, 128), i32),
-        in_specs=[smem] * 4,
-        out_specs=smem,
-        name="slots",
-    )(block_aux, block_row, block_col, extents)
+    lists = jnp.pad(jnp.stack([block_aux, block_row, block_col, extents]), ((0, 4), (0, 128 - held)),
+                    constant_values=1 << 20)
     part = cap // 4
     tiles, meta, green = pl.pallas_call(
-        bind(exchange_kernel, cap),
+        bind(exchange_kernel, cap, depth // side),
         out_shape=(
             jax.ShapeDtypeStruct((4, owners, part, side, side), blocks.dtype),
             jax.ShapeDtypeStruct((owners, 8, 128), i32),
@@ -429,16 +429,18 @@
         scratch_shapes=[
             pltpu.VMEM(blocks.shape, blocks.dtype),
             pltpu.VMEM((width, depth), occ_green.dtype),
-            pltpu.SMEM((owners, 8, 128), i32),
+            pltpu.VMEM((8, 128), i32),
+            pltpu.VMEM((8, 128), i32),
+            pltpu.SMEM((8, 128), i32),
             pltpu.VMEM((owners, 8, 128), i32),
             pltpu.VMEM((7, part, side, side), blocks.dtype),
             dma((5,)),
             dma((7,)), dma((7,)), dma((7,)), dma((7,)), dma((8,)), dma((8,)), dma((16,)), dma((16,)),
             dma(()), dma(()),
         ],
-        compiler_params=pltpu.CompilerParams(collective_id=0, has_side_effects=True, vmem_limit_bytes=VMEM_LIMIT),
+        compiler_params=pltpu.CompilerParams(collective_id=0, has_side_effects=True, vmem_limit_bytes=59 * 1024 * 1024),
         name="exchange",
-    )(codes, blocks, occ_green.T, virt_green.T)
+    )(lists, blocks, occ_green.T, virt_green.T)
     total = pl.pallas_call(
         bind(product_kernel, cap),
         out_shape=jax.ShapeDtypeStruct((NP, side, 2 * width), f32),

time: 89.7 us -> 83.7 us (0.933)
  Pallas kernels: 84 us -> 77.6 us
    pallas_call x2 -> x1, Pallas kernels: 38.1 us -> 32.5 us  [on_slice(): pl.pallas_call(bind(exchange_kernel, cap, depth // side), out_shape=(jax....]
    unnamed x9 -> x7, local copies, waits for them, and re-layouts: 5.42 us -> 4.56 us
where the time goes in v4:
time: 83.7 us; the launch traced here: 83.5 us
  Pallas kernels  77.6 us (93%)
  local copies, waits for them, and re-layouts  5.16 us (6%)
    pallas_call x1, Pallas kernels, on_slice(): pl.pallas_call(pair_kernel, out_shape=jax.ShapeDtypeStruct((NP, NP), f32)...  39.5 us
    pallas_call x1, Pallas kernels, on_slice(): pl.pallas_call(bind(exchange_kernel, cap, depth // side), out_shape=(jax....  32.5 us
    pallas_call x1, Pallas kernels, on_slice(): pl.pallas_call(bind(product_kernel, cap), out_shape=jax.ShapeDtypeStruct(...  5.63 us
    unnamed x7, local copies, waits for them, and re-layouts  4.56 us

profile of v4, /device:TPU:0, one launch (start us, length us, event | category | flops | bytes accessed | tf_op | source)
XLA Modules:
  0.0 83.5 jit_solution(1828752303417079036)
XLA Ops:
  0.0 0.7 pad_add_fusion
  0.7 0.6 pad.4.refs_0_
  1.3 32.5 %exchange.1 = (bf16[4,8,3,128,128]{4,3,2,1,0:T(8,128)(2,1)}, s32[8,8,128]{2,1,0:T(8,128)}, bf16[128,5120]{1,0:T(8,128)(2,1)}) custom-call(s32[8,128]{1,0:T(8,128)} %pad.4.refs_0_, bf16[88,128,128]{2,1,0:T(8,128)(2,1)} %refs_1_.1, bf16[64,5120]{1,0:T(8,128)(2,1)} %bitcast.6, bf16[64,5120]{1,0:T(8,128)(2,1)} %bitcast.7), custom_call_target="tpu_custom_call" | custom-call | tf_op jit(solution)/shard_map/exchange/pallas_call | solution.py:420
  33.8 0.0 copy-start
  33.8 1.9 %copy-done = bf16[4,8,3,128,128]{4,3,2,1,0:T(8,128)(2,1)S(1)} copy-done((bf16[4,8,3,128,128]{4,3,2,1,0:T(8,128)(2,1)S(1)}, bf16[4,8,3,128,128]{4,3,2,1,0:T(8,128)(2,1)}, u32[]{:S(2)}) %copy-start) | copy-done | bytes 3145752
  35.7 0.0 copy-start.1
  35.7 1.3 %copy-done.1 = bf16[128,5120]{1,0:T(8,128)(2,1)S(1)} copy-done((bf16[128,5120]{1,0:T(8,128)(2,1)S(1)}, bf16[128,5120]{1,0:T(8,128)(2,1)}, u32[]{:S(2)}) %copy-start.1) | copy-done | bytes 1310744
  37.0 0.0 copy-start.2
  37.0 0.8 copy-done.2
  37.7 5.6 %product.1.total_ref = f32[24,128,128]{2,1,0:T(8,128)S(1)} custom-call(s32[8,8,128]{2,1,0:T(8,128)S(1)} %copy-done.2, bf16[4,8,3,128,128]{4,3,2,1,0:T(8,128)(2,1)S(1)} %copy-done, bf16[128,5120]{1,0:T(8,128)(2,1)S(1)} %copy-done.1), custom_call_target="tpu_custom_call" | custom-call | tf_op jit(solution)/shard_map/product/pallas_call | solution.py:444
  43.4 39.5 %pair.1 = f32[24,24]{1,0:T(8,128)S(1)} custom-call(f32[24,128,128]{2,1,0:T(8,128)S(1)} %product.1.total_ref), custom_call_target="tpu_custom_call" | custom-call | tf_op jit(solution)/shard_map/pair/pallas_call | solution.py:453
  82.9 0.6 copy.9
Async XLA Ops:
  33.8 1.9 %copy-start = (bf16[4,8,3,128,128]{4,3,2,1,0:T(8,128)(2,1)S(1)}, bf16[4,8,3,128,128]{4,3,2,1,0:T(8,128)(2,1)}, u32[]{:S(2)}) copy-start(bf16[4,8,3,128,128]{4,3,2,1,0:T(8,128)(2,1)} %get-tuple-element.9.refs_1_) | copy-start | bytes 9437188
  35.7 1.3 %copy-start.1 = (bf16[128,5120]{1,0:T(8,128)(2,1)S(1)}, bf16[128,5120]{1,0:T(8,128)(2,1)}, u32[]{:S(2)}) copy-start(bf16[128,5120]{1,0:T(8,128)(2,1)} %get-tuple-element.10.refs_2_) | copy-start | bytes 3932164
  37.0 0.8 copy-start.2

commit v5 on v4

--- a/solution.py
+++ b/solution.py
@@ -7,8 +7,8 @@
 
 NP = 24
 MESH = pl.DeviceIdType.MESH
-VMEM_LIMIT = 40 * 1024 * 1024
-STEPS = 8
+VMEM_LIMIT = 59 * 1024 * 1024
+STEPS = 12
 OFFSETS = ((1, 0), (0, 3), (0, 1), (1, 2), (1, 1), (1, 3), (0, 2))
 
 
@@ -167,18 +167,28 @@
         to_core[8 + k].wait()
 
 
-def product_kernel(cap, meta_ref, tiles_ref, green_ref, total_ref):
+def product_kernel(cap, meta_ref, tiles_hbm, green_hbm, total_ref, tiles_ref, green_ref, load_sem):
     part = cap // 4
     side = tiles_ref.shape[-1]
+    load_green = pltpu.make_async_copy(green_hbm, green_ref, load_sem.at[4])
+    load_green.start()
+    loads = [pltpu.make_async_copy(tiles_hbm.at[q], tiles_ref.at[q], load_sem.at[q]) for q in range(4)]
+    for load in loads:
+        load.start()
     total_ref[...] = jnp.zeros_like(total_ref)
+    load_green.wait()
 
     def add_all(flipped):
-        @pl.loop(0, tiles_ref.shape[0] * tiles_ref.shape[1] // 2)
+        for quarter in range(4):
+            loads[quarter].wait()
+            add_quarter(flipped, quarter)
+
+    def add_quarter(flipped, quarter):
+        @pl.loop(0, tiles_ref.shape[1] // 2)
         def _(i):
             terms = []
             for h in range(2):
-                n = 2 * i + h
-                quarter, source = n // tiles_ref.shape[1], n % tiles_ref.shape[1]
+                source = 2 * i + h
                 for j in range(part):
                     code = meta_ref[source, 0, quarter * part + j]
                     start = pl.multiple_of((code % 256) * side, side)
@@ -194,7 +204,7 @@
     pl.when(core == 1)(lambda: add_all(True))
 
 
-def pair_kernel(total_ref, chi_ref, right_in, left_in, done, occ_in, virt_in, plane_in, line_in,
+def pair_kernel(total_hbm, chi_ref, total_ref, load_sem, right_in, left_in, done, occ_in, virt_in, plane_in, line_in,
                 right_send, right_recv, left_send, left_recv, occ_send, occ_recv, virt_send, virt_recv,
                 plane_send, plane_recv, line_send, line_recv):
     y, core, x, z = place()
@@ -211,12 +221,15 @@
         return (2 * (number // 4) + number % 2, (number // 2) % 2, z)
 
     mine = 4 * y + 2 * x + core
+    load_total = pltpu.make_async_copy(total_hbm, total_ref, load_sem)
+    load_total.start()
     barrier = pltpu.get_barrier_semaphore()
     for k in range(1, 4):
         pl.semaphore_signal(barrier, inc=1, device_id=(row, x, (z + k) % 4), device_id_type=MESH)
     for k in range(1, 8):
         pl.semaphore_signal(barrier, inc=1, device_id=device((mine + k) % 8), device_id_type=MESH)
     pl.semaphore_wait(barrier, 10)
+    load_total.wait()
 
     def chunk(c):
         return pl.ds(c * size, size)
@@ -270,7 +283,7 @@
             def _():
                 virt_copy(c, 1).start()
 
-    lag = 6
+    lag = 7
 
     @pl.when(z == 0)
     def _():
@@ -303,11 +316,11 @@
             left(c, total_ref.at[chunk(c), :rows]).wait_send()
 
     def relay(near, far):
-        for c in range(steps + 2):
+        for c in range(steps + 3):
             if c < steps:
                 near(c)
-            if c >= 2:
-                far(c - 2)
+            if c >= 3:
+                far(c - 3)
 
     pl.when(z == 1)(lambda: relay(pass_right, pass_left))
     pl.when(z == 2)(lambda: relay(pass_left, pass_right))
@@ -438,14 +451,19 @@
             dma((7,)), dma((7,)), dma((7,)), dma((7,)), dma((8,)), dma((8,)), dma((16,)), dma((16,)),
             dma(()), dma(()),
         ],
-        compiler_params=pltpu.CompilerParams(collective_id=0, has_side_effects=True, vmem_limit_bytes=59 * 1024 * 1024),
+        compiler_params=pltpu.CompilerParams(collective_id=0, has_side_effects=True, vmem_limit_bytes=VMEM_LIMIT),
         name="exchange",
     )(lists, blocks, occ_green.T, virt_green.T)
     total = pl.pallas_call(
         bind(product_kernel, cap),
         out_shape=jax.ShapeDtypeStruct((NP, side, 2 * width), f32),
-        in_specs=[smem, vmem, vmem],
+        in_specs=[smem, pl.BlockSpec(memory_space=pl.ANY), pl.BlockSpec(memory_space=pl.ANY)],
         out_specs=vmem,
+        scratch_shapes=[
+            pltpu.VMEM((4, owners, part, side, side), blocks.dtype),
+            pltpu.VMEM((2 * width, depth), occ_green.dtype),
+            dma((5,)),
+        ],
         compiler_params=pltpu.CompilerParams(vmem_limit_bytes=VMEM_LIMIT),
         name="product",
     )(meta, tiles, green)
@@ -453,9 +471,11 @@
     return pl.pallas_call(
         pair_kernel,
         out_shape=jax.ShapeDtypeStruct((NP, NP), f32),
-        in_specs=[vmem],
+        in_specs=[pl.BlockSpec(memory_space=pl.ANY)],
         out_specs=vmem,
         scratch_shapes=[
+            pltpu.VMEM((NP, side, side), f32),
+            dma(()),
             pltpu.VMEM((NP, rows, side), f32),
             pltpu.VMEM((NP, rows, side), f32),
             pltpu.VMEM((NP, rows, side), f32),

time: 83.7 us -> 82.7 us (0.988)
  local copies, waits for them, and re-layouts: 5.16 us -> 1.91 us
  Pallas kernels: 77.6 us -> 79.8 us
    unnamed x7 -> x1, local copies, waits for them, and re-layouts: 4.56 us -> 1.31 us
    pallas_call x1, Pallas kernels: 5.63 us -> 8.24 us  [on_slice(): pl.pallas_call(bind(product_kernel, cap), out_shape=jax.ShapeDtypeStruct(...]
where the time goes in v5:
time: 82.7 us; the launch traced here: 82.4 us
  Pallas kernels  79.8 us (96%)
  local copies, waits for them, and re-layouts  1.91 us (2%)
    pallas_call x1, Pallas kernels, on_slice(): pl.pallas_call(pair_kernel, out_shape=jax.ShapeDtypeStruct((NP, NP), f32)...  39 us
    pallas_call x1, Pallas kernels, on_slice(): pl.pallas_call(bind(exchange_kernel, cap, depth // side), out_shape=(jax....  32.6 us
    pallas_call x1, Pallas kernels, on_slice(): pl.pallas_call(bind(product_kernel, cap), out_shape=jax.ShapeDtypeStruct(...  8.24 us

profile of v5, /device:TPU:0, one launch (start us, length us, event | category | flops | bytes accessed | tf_op | source)
XLA Modules:
  0.0 82.4 jit_solution(8928890054139045883)
XLA Ops:
  0.0 0.7 pad_add_fusion
  0.7 0.6 pad.4.refs_0_
  1.3 32.6 %exchange.1 = (bf16[4,8,3,128,128]{4,3,2,1,0:T(8,128)(2,1)}, s32[8,8,128]{2,1,0:T(8,128)}, bf16[128,5120]{1,0:T(8,128)(2,1)}) custom-call(s32[8,128]{1,0:T(8,128)} %pad.4.refs_0_, bf16[88,128,128]{2,1,0:T(8,128)(2,1)} %refs_1_.1, bf16[64,5120]{1,0:T(8,128)(2,1)} %bitcast.6, bf16[64,5120]{1,0:T(8,128)(2,1)} %bitcast.7), custom_call_target="tpu_custom_call" | custom-call | tf_op jit(solution)/shard_map/exchange/pallas_call | solution.py:433
  33.9 8.2 %product.1.total_hbm = f32[24,128,128]{2,1,0:T(8,128)} custom-call(s32[8,8,128]{2,1,0:T(8,128)} %get-tuple-element.8.refs_0_, bf16[4,8,3,128,128]{4,3,2,1,0:T(8,128)(2,1)} %get-tuple-element.9.refs_1_, bf16[128,5120]{1,0:T(8,128)(2,1)} %get-tuple-element.10.refs_2_), custom_call_target="tpu_custom_call" | custom-call | tf_op jit(solution)/shard_map/product/pallas_call | solution.py:457
  42.1 39.0 %pair.1 = f32[24,24]{1,0:T(8,128)} custom-call(f32[24,128,128]{2,1,0:T(8,128)} %product.1.total_hbm), custom_call_target="tpu_custom_call" | custom-call | tf_op jit(solution)/shard_map/pair/pallas_call | solution.py:471
  81.1 1.3 %copy.9 = f32[24,24]{1,0:T(8,128)} copy(f32[24,24]{1,0:T(8,128)} %pair.1) | data formatting | bytes 4608

commit v6 on v5

--- a/solution.py
+++ b/solution.py
@@ -147,12 +147,12 @@
         tile_copies[k].wait_recv()
         to_y[k] = forward(row, sources[k], y_send, y_recv, k, across)
         to_core[k] = forward(row, sources[k], core_send, core_recv, k, sibling)
-        if k >= 1:
-            e = order[k - 1]
+        if k >= 3:
+            e = order[k - 3]
             to_y[e].wait_recv()
             to_core[8 + e] = forward(across, sources[e], core_send, core_recv, 8 + e, sibling)
 
-    for e in order[6:]:
+    for e in order[4:]:
         to_y[e].wait_recv()
         to_core[8 + e] = forward(across, sources[e], core_send, core_recv, 8 + e, sibling)
     load_own(occ_hbm).wait()
@@ -289,30 +289,30 @@
     def _():
         for c in range(steps + lag):
             if c < steps:
-                if c >= 3:
-                    right(c - 3, total_ref.at[chunk(c - 3), rows:]).wait_send()
+                if c >= 5:
+                    right(c - 5, total_ref.at[chunk(c - 5), rows:]).wait_send()
                 right(c, total_ref.at[chunk(c), rows:]).start()
             if c >= lag:
                 e = c - lag
                 left(e, left_in.at[chunk(e)]).wait_recv()
                 done[chunk(e)] = left_in[chunk(e)] + total_ref[chunk(e), :rows]
                 hand_out(e)
-        for c in range(steps - 3, steps):
+        for c in range(steps - 5, steps):
             right(c, total_ref.at[chunk(c), rows:]).wait_send()
 
     @pl.when(z == 3)
     def _():
         for c in range(steps + lag):
             if c < steps:
-                if c >= 3:
-                    left(c - 3, total_ref.at[chunk(c - 3), :rows]).wait_send()
+                if c >= 5:
+                    left(c - 5, total_ref.at[chunk(c - 5), :rows]).wait_send()
                 left(c, total_ref.at[chunk(c), :rows]).start()
             if c >= lag:
                 e = c - lag
                 right(e, right_in.at[chunk(e)]).wait_recv()
                 done[chunk(e)] = right_in[chunk(e)] + total_ref[chunk(e), rows:]
                 hand_out(e)
-        for c in range(steps - 3, steps):
+        for c in range(steps - 5, steps):
             left(c, total_ref.at[chunk(c), :rows]).wait_send()
 
     def relay(near, far):
@@ -486,7 +486,7 @@
             dma((STEPS,)), dma((STEPS,)), dma((STEPS,)), dma((STEPS,)), dma((STEPS,)), dma((STEPS,)),
             dma((STEPS, 2)), dma((STEPS,)), dma((8,)), dma((8,)), dma((4,)), dma((2,)),
         ],
-        compiler_params=pltpu.CompilerParams(collective_id=1, has_side_effects=True, vmem_limit_bytes=VMEM_LIMIT),
+        compiler_params=pltpu.CompilerParams(collective_id=1, has_side_effects=True, vmem_limit_bytes=53 * 1024 * 1024),
         name="pair",
     )(total)
 

time: 82.7 us -> 81.3 us (0.983)
  no operation moved by 1% of the time
where the time goes in v6:
time: 81.3 us; the launch traced here: 81.1 us
  Pallas kernels  79.2 us (97%)
  local copies, waits for them, and re-layouts  1.2 us (1%)
    pallas_call x1, Pallas kernels, on_slice(): pl.pallas_call(pair_kernel, out_shape=jax.ShapeDtypeStruct((NP, NP), f32)...  38.4 us
    pallas_call x1, Pallas kernels, on_slice(): pl.pallas_call(bind(exchange_kernel, cap, depth // side), out_shape=(jax....  32.6 us
    pallas_call x1, Pallas kernels, on_slice(): pl.pallas_call(bind(product_kernel, cap), out_shape=jax.ShapeDtypeStruct(...  8.24 us

profile of v6, /device:TPU:0, one launch (start us, length us, event | category | flops | bytes accessed | tf_op | source)
XLA Modules:
  0.0 81.1 jit_solution(6789771356540872951)
XLA Ops:
  0.0 0.7 pad_add_fusion
  0.7 0.6 pad.4.refs_0_
  1.3 32.6 %exchange.1 = (bf16[4,8,3,128,128]{4,3,2,1,0:T(8,128)(2,1)}, s32[8,8,128]{2,1,0:T(8,128)}, bf16[128,5120]{1,0:T(8,128)(2,1)}) custom-call(s32[8,128]{1,0:T(8,128)} %pad.4.refs_0_, bf16[88,128,128]{2,1,0:T(8,128)(2,1)} %refs_1_.1, bf16[64,5120]{1,0:T(8,128)(2,1)} %bitcast.6, bf16[64,5120]{1,0:T(8,128)(2,1)} %bitcast.7), custom_call_target="tpu_custom_call" | custom-call | tf_op jit(solution)/shard_map/exchange/pallas_call | solution.py:433
  33.9 8.2 %product.1.total_hbm = f32[24,128,128]{2,1,0:T(8,128)} custom-call(s32[8,8,128]{2,1,0:T(8,128)} %get-tuple-element.8.refs_0_, bf16[4,8,3,128,128]{4,3,2,1,0:T(8,128)(2,1)} %get-tuple-element.9.refs_1_, bf16[128,5120]{1,0:T(8,128)(2,1)} %get-tuple-element.10.refs_2_), custom_call_target="tpu_custom_call" | custom-call | tf_op jit(solution)/shard_map/product/pallas_call | solution.py:457
  42.1 38.4 %pair.1 = f32[24,24]{1,0:T(8,128)S(1)} custom-call(f32[24,128,128]{2,1,0:T(8,128)} %product.1.total_hbm), custom_call_target="tpu_custom_call" | custom-call | tf_op jit(solution)/shard_map/pair/pallas_call | solution.py:471
  80.5 0.6 copy.9

commit v7 on v6

--- a/solution.py
+++ b/solution.py
@@ -117,7 +117,7 @@
     sources = [owner_of(peer) for peer in peers] + [me]
     order = [7] + list(range(7))
     to_y, to_core = {}, {}
-    window = 4
+    window = 5
     load_codes.wait()
     load_blocks.wait()
 
@@ -184,11 +184,11 @@
             add_quarter(flipped, quarter)
 
     def add_quarter(flipped, quarter):
-        @pl.loop(0, tiles_ref.shape[1] // 2)
+        @pl.loop(0, tiles_ref.shape[1] // 4)
         def _(i):
             terms = []
-            for h in range(2):
-                source = 2 * i + h
+            for h in range(4):
+                source = 4 * i + h
                 for j in range(part):
                     code = meta_ref[source, 0, quarter * part + j]
                     start = pl.multiple_of((code % 256) * side, side)

time: 81.3 us -> 80.3 us (0.988)
  Pallas kernels: 79.2 us -> 78.1 us
    pallas_call x1, Pallas kernels: 8.24 us -> 7.17 us  [on_slice(): pl.pallas_call(bind(product_kernel, cap), out_shape=jax.ShapeDtypeStruct(...]
where the time goes in v7:
time: 80.3 us; the launch traced here: 80 us
  Pallas kernels  78.1 us (97%)
  local copies, waits for them, and re-layouts  1.2 us (1%)
    pallas_call x1, Pallas kernels, on_slice(): pl.pallas_call(pair_kernel, out_shape=jax.ShapeDtypeStruct((NP, NP), f32)...  38.4 us
    pallas_call x1, Pallas kernels, on_slice(): pl.pallas_call(bind(exchange_kernel, cap, depth // side), out_shape=(jax....  32.6 us
    pallas_call x1, Pallas kernels, on_slice(): pl.pallas_call(bind(product_kernel, cap), out_shape=jax.ShapeDtypeStruct(...  7.17 us

profile of v7, /device:TPU:0, one launch (start us, length us, event | category | flops | bytes accessed | tf_op | source)
XLA Modules:
  0.0 80.0 jit_solution(7281103135746484323)
XLA Ops:
  0.0 0.7 pad_add_fusion
  0.7 0.6 pad.4.refs_0_
  1.3 32.6 %exchange.1 = (bf16[4,8,3,128,128]{4,3,2,1,0:T(8,128)(2,1)}, s32[8,8,128]{2,1,0:T(8,128)}, bf16[128,5120]{1,0:T(8,128)(2,1)}) custom-call(s32[8,128]{1,0:T(8,128)} %pad.4.refs_0_, bf16[88,128,128]{2,1,0:T(8,128)(2,1)} %refs_1_.1, bf16[64,5120]{1,0:T(8,128)(2,1)} %bitcast.6, bf16[64,5120]{1,0:T(8,128)(2,1)} %bitcast.7), custom_call_target="tpu_custom_call" | custom-call | tf_op jit(solution)/shard_map/exchange/pallas_call | solution.py:433
  33.9 7.2 %product.1.total_hbm = f32[24,128,128]{2,1,0:T(8,128)} custom-call(s32[8,8,128]{2,1,0:T(8,128)} %get-tuple-element.8.refs_0_, bf16[4,8,3,128,128]{4,3,2,1,0:T(8,128)(2,1)} %get-tuple-element.9.refs_1_, bf16[128,5120]{1,0:T(8,128)(2,1)} %get-tuple-element.10.refs_2_), custom_call_target="tpu_custom_call" | custom-call | tf_op jit(solution)/shard_map/product/pallas_call | solution.py:457
  41.1 38.4 %pair.1 = f32[24,24]{1,0:T(8,128)S(1)} custom-call(f32[24,128,128]{2,1,0:T(8,128)} %product.1.total_hbm), custom_call_target="tpu_custom_call" | custom-call | tf_op jit(solution)/shard_map/pair/pallas_call | solution.py:471
  79.4 0.6 copy.9
